TPU v7x, 256 devices: a whole 4x4x8 slice. The times are simulated.
256 devices in a mesh: ctx: 16 (over x, y_lo, core), tp: 16 (over z, y_hi).
Axes of the slice: x: 4, y: 4 (y_hi: 2, y_lo: 2; y = y_hi * 2 + y_lo), z: 8, core: 2. Of those that a mesh axis runs over, the one named last changes fastest.
Arguments:
- queries: bfloat16 [4096, 8192], P('ctx', 'tp'), may hold values from -5 to 5
- keys: bfloat16 [8, 4096, 128], P(None, 'ctx'), may hold values from -5 to 5
- values: bfloat16 [8, 4096, 128], P(None, 'ctx'), may hold values from -6 to 6
- d_out: bfloat16 [4096, 8192], P('ctx', 'tp'), may hold values from -6 to 6
- span_order: int32 [32], replicated, may hold values from 0 to 31, each once
- segments: int32 [4096], replicated, may hold values from 0 to 3, never falling along the last dimension, each value on 1 to 2048 neighbouring positions
Outputs:
- d_queries: bfloat16 [4096, 8192], P('ctx', 'tp')
- d_keys: float32 [8, 4096, 128], P(None, 'ctx')
- d_values: float32 [8, 4096, 128], P(None, 'ctx')
Inputs may be any that keep to these rules, and one draw needn't show every extreme that they name: `span_order`: each number once. `segments`: never falling along positions.
All inputs are finite; a program needn't handle non-finite values.
Results may differ from a plain program's by a relative error of at most 0.015.
Values may be sent and summed in bfloat16 or wider, within the bound.
A program may use at most 64 MiB of HBM per device.

v0:
```python
import jax
import jax.numpy as jnp
from jax import lax
from jax.sharding import PartitionSpec as P

GROUP = 8


NEGATIVE = -1e30


def block_scores(
    query_rows, whole_keys, key_pos, key_seg, query_pos, query_seg, start, block, scale
):
    key_block = lax.dynamic_slice_in_dim(whole_keys, start, block, 0)
    pos_block = lax.dynamic_slice_in_dim(key_pos, start, block, 0)
    seg_block = lax.dynamic_slice_in_dim(key_seg, start, block, 0)
    allowed = (pos_block[None, :] <= query_pos[:, None]) & (
        seg_block[None, :] == query_seg[:, None]
    )
    scores = (
        jnp.einsum("qhd,kd->hqk", query_rows, key_block, preferred_element_type=jnp.float32) * scale
    )
    return (jnp.where(allowed[None], scores, NEGATIVE), allowed, key_block)


def per_device(queries, keys, values, d_out, span_order, segments):
    rows_dev = queries.shape[0]
    span = rows_dev // 2
    head_dim = keys.shape[2]
    q_heads = queries.shape[1] // head_dim
    scale = head_dim ** (-0.5)
    tp_index = lax.axis_index("tp")
    ctx_index = lax.axis_index("ctx")
    kv_index = tp_index * q_heads // GROUP
    own_keys = lax.dynamic_index_in_dim(keys, kv_index, 0, keepdims=False)
    own_values = lax.dynamic_index_in_dim(values, kv_index, 0, keepdims=False)
    whole_keys, whole_values = (
        lax.all_gather(own_keys, "ctx", axis=0, tiled=True),
        lax.all_gather(own_values, "ctx", axis=0, tiled=True),
    )
    tokens = whole_keys.shape[0]
    all_rows = jnp.arange(tokens, dtype=jnp.int32)
    key_pos = span_order[all_rows // span] * span + all_rows % span
    key_seg = segments[key_pos]
    my_rows = ctx_index * rows_dev + jnp.arange(rows_dev, dtype=jnp.int32)
    query_pos = span_order[my_rows // span] * span + my_rows % span
    query_seg = segments[query_pos]
    block = min(512, tokens)
    count = tokens // block
    query_rows = queries.reshape(rows_dev, q_heads, head_dim)
    grad_rows = d_out.reshape(rows_dev, q_heads, head_dim)
    steps_idx = jnp.arange(count, dtype=jnp.int32)

    def scores_at(index):
        return block_scores(
            query_rows,
            whole_keys,
            key_pos,
            key_seg,
            query_pos,
            query_seg,
            index * block,
            block,
            scale,
        )

    def stats_step(carry, index):
        run_max, run_sum = carry
        scores, allowed, key_block = scores_at(index)
        new_max = jnp.maximum(run_max, jnp.max(scores, axis=-1))
        weights = jnp.where(allowed[None], jnp.exp(scores - new_max[..., None]), 0.0)
        run_sum = run_sum * jnp.exp(run_max - new_max) + jnp.sum(weights, axis=-1)
        return ((new_max, run_sum), None)

    start_max = jnp.full((q_heads, rows_dev), NEGATIVE, jnp.float32)
    start_sum = jnp.zeros((q_heads, rows_dev), jnp.float32)
    (run_max, run_sum), unused = lax.scan(stats_step, (start_max, start_sum), steps_idx)
    lse = run_max + jnp.log(run_sum)

    def output_step(total, index):
        scores, allowed, key_block = scores_at(index)
        probs16 = jnp.exp(scores - lse[..., None]).astype(jnp.bfloat16)
        value_block = lax.dynamic_slice_in_dim(whole_values, index * block, block, 0)
        return (
            total
            + jnp.einsum("hqk,kd->qhd", probs16, value_block, preferred_element_type=jnp.float32),
            None,
        )

    output, unused = lax.scan(
        output_step, jnp.zeros((rows_dev, q_heads, head_dim), jnp.float32), steps_idx
    )
    delta = jnp.sum(grad_rows.astype(jnp.float32) * output, axis=-1).T

    def grad_step(dq_total, index):
        scores, allowed, key_block = scores_at(index)
        value_block = lax.dynamic_slice_in_dim(whole_values, index * block, block, 0)
        probs = jnp.exp(scores - lse[..., None])
        probs16 = probs.astype(jnp.bfloat16)
        dprobs = jnp.einsum(
            "qhd,kd->hqk", grad_rows, value_block, preferred_element_type=jnp.float32
        )
        dscores = (probs * (dprobs - delta[..., None])).astype(jnp.bfloat16)
        dq_total = dq_total + jnp.einsum(
            "hqk,kd->qhd", dscores, key_block, preferred_element_type=jnp.float32
        )
        dkey_block = (
            jnp.einsum("hqk,qhd->kd", dscores, query_rows, preferred_element_type=jnp.float32)
            * scale
        )
        dvalue_block = jnp.einsum(
            "hqk,qhd->kd", probs16, grad_rows, preferred_element_type=jnp.float32
        )
        return (dq_total, (dkey_block, dvalue_block))

    dq_total, (dkey_blocks, dvalue_blocks) = lax.scan(
        grad_step, jnp.zeros((rows_dev, q_heads, head_dim), jnp.float32), steps_idx
    )
    d_queries = (dq_total * scale).astype(jnp.bfloat16).reshape(rows_dev, q_heads * head_dim)
    dkey_terms = dkey_blocks.reshape(tokens, head_dim)
    dvalue_terms = dvalue_blocks.reshape(tokens, head_dim)
    tp_size = lax.axis_size("tp")
    terms = jnp.concatenate([dkey_terms, dvalue_terms], axis=1)
    mine = lax.psum_scatter(
        terms.astype(jnp.bfloat16), "ctx", scatter_dimension=0, tiled=True
    ).astype(jnp.float32)
    every = lax.all_gather(mine[None].astype(jnp.bfloat16), "tp", axis=0, tiled=True).astype(
        jnp.float32
    )
    share = GROUP // q_heads
    summed = jnp.sum(every.reshape(tp_size // share, share, rows_dev, 2 * head_dim), axis=1)
    d_keys = summed[..., :head_dim]
    d_values = summed[..., head_dim:]
    return (d_queries, d_keys, d_values)


def solution(mesh):
    return jax.shard_map(
        per_device,
        mesh=mesh,
        in_specs=(
            P("ctx", "tp"),
            P(None, "ctx", None),
            P(None, "ctx", None),
            P("ctx", "tp"),
            P(),
            P(),
        ),
        out_specs=(P("ctx", "tp"), P(None, "ctx", None), P(None, "ctx", None)),
        check_vma=False,
    )
```

profile of v0, /device:TPU:8, one launch (start us, length us, event | category | flops | bytes accessed | tf_op | source)
XLA Modules:
  0.0 463.7 jit_solution(13663045603511993076)
XLA Ops:
  10.4 1.8 fusion.57
  12.3 2.1 fusion.56
  15.8 4.4 compare_select_fusion.2
  20.2 4.4 compare_select_fusion.10
  27.2 16.2 %fusion.48 = (s32[4096]{0:T(1024)}, s32[4096]{0:T(1024)S(1)}) fusion(pred[4096]{0:T(1024)(128)(4,1)S(1)} %compare_reduce_fusion, pred[4096]{0:T(1024)(128)(4,1)S(1)} %compare_reduce_fusion.1, pred[4096]{0:T(1024)(128)(4,1)S(1)} %compare_reduce_fusion.2, pred[4096]{0:T(1024)(128)(4,1)S(1)} %compare_reduce_fusion.3, ...), kind=kLoop, calls=%fused_computation.102 | loop fusion | flops 135168 | bytes 151652 | tf_op jit(solution)/shard_map/add | solution.py:44
  43.4 15.5 %fusion.53 = (s32[256]{0:T(256)S(1)}, s32[256]{0:T(256)S(1)}) fusion(s32[]{:T(128)S(6)} %mul.92, pred[256]{0:T(512)(128)(4,1)S(1)} %get-tuple-element.474, pred[256]{0:T(512)(128)(4,1)S(1)} %get-tuple-element.475, pred[256]{0:T(512)(128)(4,1)S(1)} %get-tuple-element.476, pred[256]{0:T(512)(128)(4,1)S(1)} %get-tuple-element.477, ...), kind=kLoop, calls=%fused_computation.153 | loop fusion | flops 9984 | bytes 9576 | tf_op jit(solution)/shard_map/add | solution.py:47
  59.0 40.5 %gather_fusion = s32[4096]{0:T(1024)} fusion(s32[4096]{0:T(1024)S(1)} %copy-done.1, s32[4096]{0:T(1024)S(1)} %broadcast_clamp_fusion), kind=kCustom, calls=%fused_computation | custom fusion | bytes 49152 | tf_op jit(solution)/shard_map/gather | solution.py:45
  99.5 1.7 gather_fusion.1
  102.1 54.3 %while.39 = (s32[]{:T(128)}, f32[4,256]{1,0:T(4,128)S(1)}, f32[4,256]{1,0:T(4,128)}, s32[8]{0:T(128)}, s32[4096]{0:T(1024)}, /*index=5*/s32[256]{0:T(256)S(1)}, ...) while((s32[]{:T(128)}, f32[4,256]{1,0:T(4,128)S(1)}, ...), condition=%wide.region_3.4_spmd.clone, body=%wide.region_0.3_spmd.clone.sunk | while | flops 138810368 | bytes 5048534 | solution.py:78
  157.1 48.5 %while.40 = (s32[]{:T(128)}, f32[256,4,128]{0,2,1:T(8,128)}, s32[8]{0:T(128)S(1)}, bf16[4096,128]{1,0:T(8,128)(2,1)}, s32[4096]{0:T(1024)}, /*index=5*/s32[256]{...) while((s32[]{:T(128)}, f32[256,4,128]{0,2,1:T(8,128)}, ...), condition=%wide.region_5.6_spmd.clone, body=%wide.region_4.5_spmd.clone.sunk | while | flops 271187968 | bytes 1855192 | solution.py:91
  160.1 2.8 fusion.93
  166.1 3.0 fusion.93
  172.1 3.0 fusion.93
  178.2 3.0 fusion.93
  184.3 3.0 fusion.93
  190.4 3.0 fusion.93
  196.4 3.0 fusion.93
  202.5 3.0 fusion.93
  206.7 88.4 %while.41 = (s32[]{:T(128)}, f32[256,4,128]{0,2,1:T(8,128)S(1)}, bf16[8,512,128]{2,1,0:T(8,128)(2,1)}, bf16[8,512,128]{2,1,0:T(8,128)(2,1)}, s32[8]{0:T(128)S(1)...) while((s32[]{:T(128)}, f32[256,4,128]{0,2,1:T(8,128)S(1)}, ...), condition=%wide.region_8.9_spmd.clone, body=%wide.region_7.8_spmd.clone.sunk | while | flops 675479552 | bytes 29515068 | solution.py:117
  209.6 1.5 fusion.104
  220.7 1.5 fusion.104
  231.7 1.5 fusion.104
  242.8 1.5 fusion.104
  253.8 1.5 fusion.104
  264.9 1.5 fusion.104
  275.9 1.5 fusion.104
  287.0 1.5 fusion.104
  295.1 3.1 pad_maximum_fusion
  298.3 65.4 %reduce-scatter.2.cloned.1.call-done = bf16[256,256]{1,0:T(8,128)(2,1)} async-done(((bf16[4096,256]{1,0:T(8,128)(2,1)}), bf16[256,256]{1,0:T(8,128)(2,1)}) %reduce-scatter.2.cloned.1.call-update) | async-done | bytes 131088 | tf_op jit(solution)/shard_map/reduce_scatter | solution.py:125
  364.6 88.8 %all-gather.11.cloned.1.call-done = bf16[4096,256]{1,0:T(8,128)(2,1)} async-done(((bf16[256,256]{1,0:T(8,128)(2,1)}), bf16[4096,256]{1,0:T(8,128)(2,1)}) %all-gather.11.cloned.1.call-update) | async-done | bytes 2097168 | tf_op jit(solution)/shard_map/all_gather | solution.py:128
  453.3 2.2 convert_reduce_fusion
  455.6 1.5 fusion.55
  (280 shorter events, 148.6 us)
Async XLA Ops:
  7.2 1.0 copy-start
  7.2 51.8 %copy-start.1 = (s32[4096]{0:T(1024)S(1)}, s32[4096]{0:T(1024)}, u32[]{:S(2)}) copy-start(s32[4096]{0:T(1024)} %param.17) | copy-start | bytes 49156
  7.2 94.4 %all-gather.7.cloned.1.call-start = ((), (), s32[]{:S(2)}) async-start(), calls=%async_computation.2 | async-start | bytes 1114112 | tf_op jit(solution)/shard_map/all_gather | solution.py:39
  8.9 148.2 %all-gather.9.cloned.1.call-start = ((), (), s32[]{:S(2)}) async-start(), calls=%async_computation.3 | async-start | bytes 1114112 | tf_op jit(solution)/shard_map/all_gather | solution.py:40
  10.4 353.2 %reduce-scatter.2.cloned.1.call-start = ((), (), s32[]{:S(2)}) async-start(), calls=%async_computation.1 | async-start | bytes 2228224 | tf_op jit(solution)/shard_map/reduce_scatter | solution.py:125
  59.0 42.3 %copy-start.5 = (bf16[256,512]{1,0:T(8,128)(2,1)S(1)}, bf16[256,512]{1,0:T(8,128)(2,1)}, u32[]{:S(2)}) copy-start(bf16[256,512]{1,0:T(8,128)(2,1)} %param.15) | copy-start | bytes 786436
  157.1 49.6 %copy-start.4 = (f32[256,4,128]{0,2,1:T(8,128)S(1)}, f32[256,4,128]{0,2,1:T(8,128)}, u32[]{:S(2)}) copy-start(f32[256,4,128]{0,2,1:T(8,128)} %custom-call.3) | copy-start | bytes 1572868
  211.2 1.4 copy-start.2
  215.0 1.7 copy-start.3
  222.2 1.4 copy-start.2
  226.0 1.7 copy-start.3
  233.3 1.4 copy-start.2
  237.1 1.7 copy-start.3
  244.3 1.4 copy-start.2
  248.1 1.7 copy-start.3
  255.4 1.4 copy-start.2
  259.2 1.7 copy-start.3
  266.4 1.4 copy-start.2
  270.2 1.7 copy-start.3
  277.5 1.4 copy-start.2
  281.3 1.7 copy-start.3
  288.5 1.4 copy-start.2
  292.3 1.7 copy-start.3
  298.2 155.1 %all-gather.11.cloned.1.call-start = ((), (), s32[]{:S(2)}) async-start(), calls=%async_computation.4 | async-start | bytes 2228224 | tf_op jit(solution)/shard_map/all_gather | solution.py:128
Sparse Core Ops, SparseCore 0:
  9.9 37.5 all-gather.6
  49.3 35.0 all-gather.8
  298.3 65.2 reduce-scatter.1
  366.1 87.2 all-gather.10
where the time goes:
time: 468 us; the launch traced here: 464 us
  waiting for transfers between devices  154 us (33%)
  local copies, waits for them, and re-layouts  123 us (26%)
  matrix products  87.3 us (19%)
  other arithmetic  68.2 us (15%)
  loops' own time  17.1 us (4%)
  between operations  14 us (3%)
    all_gather x1, waiting for transfers between devices, per_device(): lax.all_gather(mine[None].astype(jnp.bfloat16), 'tp', axis=0, tiled=True)  88.8 us
    reduce_scatter x1, waiting for transfers between devices, per_device(): lax.psum_scatter(terms.astype(jnp.bfloat16), 'ctx', scatter_dimension=0,...  65.4 us
    gather x1, local copies, waits for them, and re-layouts, per_device(): key_seg = segments[key_pos]  40.5 us
    dot_general x8, matrix products, output_step(): jnp.einsum('hqk,kd->qhd', probs16, value_block, preferred_element_type=jn...  24 us
    dot_general x16, matrix products, block_scores(): jnp.einsum('qhd,kd->hqk', query_rows, key_block, preferred_element_type=j...  23.4 us
    dynamic_slice x24, local copies, waits for them, and re-layouts, per_device(): lax.scan(stats_step, (start_max, start_sum), steps_idx)  19.8 us
    dynamic_slice x24, local copies, waits for them, and re-layouts, block_scores(): seg_block = lax.dynamic_slice_in_dim(key_seg, start, block, 0)  18.1 us
    dynamic_slice x24, local copies, waits for them, and re-layouts, block_scores(): pos_block = lax.dynamic_slice_in_dim(key_pos, start, block, 0)  18 us
  transfers between devices with their start and end apart: 4, of which 2 were waited for; matrix products, arithmetic and copies ran while one was open for 31% of the time, Pallas kernels for 0%

commit v1 on v0

v1 whole, which is shorter than its diff:
```python
import functools

import jax
import jax.numpy as jnp
from jax import lax
from jax.experimental import pallas as pl
from jax.experimental.pallas import tpu as pltpu
from jax.sharding import PartitionSpec as P

HD = 128
BLK = 128
HEADS_DEV = 4
COLS = HEADS_DEV * BLK
WIN = 17
NEGATIVE = -1e30
SCALE = HD**-0.5
LOG2E = 1.4426950408889634
BF = jnp.bfloat16
F32 = jnp.float32


class Place:
    def __init__(self):
        self.ctx = lax.axis_index("ctx")
        self.tp = lax.axis_index("tp")
        self.x = self.ctx // 4
        self.ylo = (self.ctx // 2) % 2
        self.core = self.ctx % 2
        self.z = self.tp // 2
        self.yhi = self.tp % 2
        self.y = self.yhi * 2 + self.ylo

    def at(self, dx=0, dy=0, dc=0, dz=0):
        x = (self.x + dx + 4) % 4
        y = (self.y + dy + 4) % 4
        c = (self.core + dc) % 2
        z = (self.z + dz + 8) % 8
        return (x * 4 + (y % 2) * 2 + c, z * 2 + y // 2)

    def block(self, dx=0, dy=0, dc=0):
        return ((self.x + dx + 4) % 4) * 4 + ((self.ylo + dy) % 2) * 2 + (self.core + dc) % 2


class Mail:
    def __init__(self, send, recv):
        self.send, self.recv, self.used, self.out = send, recv, 0, []

    def post(self, src, dst, device):
        copy = pltpu.make_async_remote_copy(
            src_ref=src,
            dst_ref=dst,
            send_sem=self.send.at[self.used],
            recv_sem=self.recv.at[self.used],
            device_id=device,
            device_id_type=pl.DeviceIdType.MESH,
        )
        self.used += 1
        copy.start()
        self.out.append(copy)
        return copy

    def drain(self):
        for copy in self.out:
            copy.wait_send()
        self.out = []


def greet(devices):
    barrier = pltpu.get_barrier_semaphore()
    for device in devices:
        pl.semaphore_signal(
            barrier, inc=1, device_id=device, device_id_type=pl.DeviceIdType.MESH
        )
    pl.semaphore_wait(barrier, len(devices))


def gather_phase(me, mail, k_ref, v_ref, kbuf, vbuf, local_sem):
    own = me.block()
    src = (k_ref.at[me.z], v_ref.at[me.z])
    buf = (kbuf, vbuf)

    def at(kind, block):
        return buf[kind].at[pl.ds(2 * block, 2)]

    def forward(kind, block, device):
        return mail.post(at(kind, block), at(kind, block), device)

    local = []
    for kind in range(2):
        copy = pltpu.make_async_copy(src[kind], at(kind, own), local_sem.at[kind])
        copy.start()
        local.append(copy)
    ydir = (1, -1)
    xp, xm, y0, s0 = [], [], [], []
    for kind in range(2):
        xp.append(mail.post(src[kind], at(kind, own), me.at(dx=1)))
        xm.append(mail.post(src[kind], at(kind, own), me.at(dx=-1)))
        y0.append(mail.post(src[kind], at(kind, own), me.at(dy=ydir[kind])))
    for kind in range(2):
        s0.append(mail.post(src[kind], at(kind, own), me.at(dc=1)))
    x2, sib, yfar = [None, None], [], []
    for kind in range(2):
        xp[kind].wait_recv()
        block = me.block(dx=-1)
        if kind == 0:
            x2[0] = forward(0, block, me.at(dx=1))
        yfar.append((kind, -1, forward(kind, block, me.at(dy=ydir[kind]))))
        sib.append(forward(kind, block, me.at(dc=1)))
        xm[kind].wait_recv()
        block = me.block(dx=1)
        if kind == 1:
            x2[1] = forward(1, block, me.at(dx=-1))
        yfar.append((kind, 1, forward(kind, block, me.at(dy=ydir[kind]))))
        sib.append(forward(kind, block, me.at(dc=1)))
    for kind in range(2):
        y0[kind].wait_recv()
        sib.append(forward(kind, me.block(dy=1), me.at(dc=1)))
    for kind in range(2):
        x2[kind].wait_recv()
        block = me.block(dx=2)
        yfar.append((kind, 2, forward(kind, block, me.at(dy=ydir[kind]))))
        sib.append(forward(kind, block, me.at(dc=1)))
    for kind, dx, copy in yfar:
        copy.wait_recv()
        sib.append(forward(kind, me.block(dx=dx, dy=1), me.at(dc=1)))
    for copy in local:
        copy.wait()
    for copy in s0 + sib:
        copy.wait_recv()
    mail.drain()


CHUNKS = ((0, 6), (6, 12), (12, 17))


def compute_phase(
    ctx, q_ref, do_ref, kbuf, vbuf, span_ref, seg_ref, dq_ref, terms,
    inv, qs, ds_rows, kg, vg, s_scr, dp_scr, p_scr, ds_scr,
):
    for j in range(32):
        found = jnp.int32(0)
        for s in range(32):
            found = found + jnp.where(span_ref[s] == j, s, 0)
        inv[j] = found
    seg_all = seg_ref[...]
    counts = [jnp.sum(jnp.where(seg_all == v, 1.0, 0.0)) for v in range(3)]
    zero = jnp.zeros((BLK, COLS), BF)
    c2 = SCALE * LOG2E

    for u in range(2):
        p = span_ref[2 * ctx + u]
        p_scr[u, WIN] = zero
        ds_scr[u, WIN] = zero
        for h in range(HEADS_DEV):
            qs[u, pl.ds(h * BLK, BLK), :] = q_ref[pl.ds(u * BLK, BLK), pl.ds(h * HD, HD)]
            ds_rows[u, pl.ds(h * BLK, BLK), :] = do_ref[pl.ds(u * BLK, BLK), pl.ds(h * HD, HD)]
        for t in range(WIN):
            j = jnp.maximum(p - (WIN - 1) + t, 0)
            s = inv[j]
            kg[pl.ds(t * BLK, BLK), :] = kbuf[s]
            vg[pl.ds(t * BLK, BLK), :] = vbuf[s]
        seg_row = seg_ref[pl.ds(p, 1), :]
        start = jnp.zeros((1, BLK), F32)
        for v in range(3):
            start = start + jnp.where(seg_row > v, counts[v], 0.0)
        first = (p - (WIN - 1)) * BLK
        start = start - first.astype(F32)
        start2 = jnp.concatenate([start, start], axis=1)
        cols2 = lax.broadcasted_iota(jnp.int32, (BLK, 2 * BLK), 1) % BLK
        rows2 = lax.broadcasted_iota(jnp.int32, (BLK, 2 * BLK), 0)
        causal = rows2 <= cols2
        rows_f = rows2.astype(F32)

        for hp in range(2):
            wide = pl.ds(hp * 256, 256)
            q2 = qs[u, wide, :]
            do2 = ds_rows[u, wide, :]
            top = jnp.full((8, 256), NEGATIVE, F32)
            for t0, t1 in CHUNKS:
                rows = pl.ds(t0 * BLK, (t1 - t0) * BLK)
                sc = lax.dot_general(
                    kg[rows, :], q2, (((1,), (1,)), ((), ())), preferred_element_type=F32
                )
                for t in range(t0, t1):
                    tile = sc[(t - t0) * BLK : (t - t0 + 1) * BLK]
                    ok = rows_f >= start2 - float(t * BLK)
                    if t == WIN - 1:
                        ok = ok & causal
                    tile = jnp.where(ok, tile * c2, NEGATIVE)
                    s_scr[pl.ds(t * BLK, BLK), wide] = tile
                    top = jnp.maximum(top, jnp.max(tile.reshape(16, 8, 256), axis=0))
            top = jnp.max(top, axis=0, keepdims=True)
            norm = jnp.zeros((8, 256), F32)
            mixed = jnp.zeros((8, 256), F32)
            for t0, t1 in CHUNKS:
                rows = pl.ds(t0 * BLK, (t1 - t0) * BLK)
                dp = lax.dot_general(
                    vg[rows, :], do2, (((1,), (1,)), ((), ())), preferred_element_type=F32
                )
                for t in range(t0, t1):
                    tile = pl.ds(t * BLK, BLK)
                    dpt = dp[(t - t0) * BLK : (t - t0 + 1) * BLK]
                    pt = jnp.exp2(s_scr[tile, wide] - top)
                    s_scr[tile, wide] = pt
                    dp_scr[tile, wide] = dpt
                    norm = norm + jnp.sum(pt.reshape(16, 8, 256), axis=0)
                    mixed = mixed + jnp.sum((pt * dpt).reshape(16, 8, 256), axis=0)
            inv_norm = 1.0 / jnp.sum(norm, axis=0, keepdims=True)
            delta = jnp.sum(mixed, axis=0, keepdims=True) * inv_norm
            dqt = jnp.zeros((HD, 256), F32)
            for t0, t1 in CHUNKS:
                for t in range(t0, t1):
                    tile = pl.ds(t * BLK, BLK)
                    prob = s_scr[tile, wide] * inv_norm
                    p_scr[u, t, :, wide] = prob.astype(BF)
                    ds_scr[u, t, :, wide] = (prob * (dp_scr[tile, wide] - delta)).astype(BF)
                rows = pl.ds(t0 * BLK, (t1 - t0) * BLK)
                dsc = ds_scr[u, pl.ds(t0, t1 - t0), :, wide].reshape((t1 - t0) * BLK, 256)
                dqt = dqt + lax.dot_general(
                    kg[rows, :], dsc, (((0,), (0,)), ((), ())), preferred_element_type=F32
                )
            for i in range(2):
                piece = (dqt[:, i * BLK : (i + 1) * BLK] * SCALE).T
                dq_ref[pl.ds(u * BLK, BLK), pl.ds((2 * hp + i) * HD, HD)] = piece.astype(BF)

    base = [span_ref[2 * ctx + u] - (WIN - 1) for u in range(2)]

    @pl.loop(0, 4)
    def _(xx):
        picks = []
        for s in range(8):
            where = span_ref[xx * 8 + s]
            pick = []
            for u in range(2):
                t = where - base[u]
                pick.append(jnp.where((t >= 0) & (t < WIN), t, WIN))
            picks.append(pick)
        for kind, source, weights in ((0, ds_scr, qs), (1, p_scr, ds_rows)):
            total = None
            for u in range(2):
                left = jnp.concatenate([source[u, picks[s][u]] for s in range(8)], axis=0)
                part = jnp.dot(left, weights[u], preferred_element_type=F32)
                total = part if total is None else total + part
            if kind == 0:
                total = total * SCALE
            terms[kind, xx] = total.astype(BF).reshape(2, 2, 2, BLK, HD)


def add_into(dst, *srcs):
    total = dst[...].astype(F32)
    for src in srcs:
        total = total + src[...].astype(F32)
    dst[...] = total.astype(BF)


def reduce_phase(me, mail, terms, part, r0, ra1, ra2, rb1, rb2, rc1, rc2, rd1, rd2, result):
    half = mail.post(terms.at[:, :, :, 1 - me.core], r0, me.at(dc=1))
    half.wait_recv()
    for kind in range(2):
        for xx in range(4):
            part[kind, xx] = (
                terms[kind, xx, :, me.core].astype(F32) + r0[kind, xx].astype(F32)
            ).astype(BF)
    x, y, ylo, yhi = me.x, me.y, me.ylo, me.yhi
    xp, xm, xo = (x + 1) % 4, (x + 3) % 4, (x + 2) % 4
    yp, ym = (y + 1) % 4, (y + 3) % 4
    hp, hm, ho = yp // 2, ym // 2, 1 - yhi
    lo = 1 - ylo
    a1p = mail.post(part.at[0, xo, :, 0], ra1.at[0], me.at(dx=1))
    a1m = mail.post(part.at[1, xo, :, 0], ra1.at[1], me.at(dx=-1))
    b1p = mail.post(part.at[ho, pl.ds(0, 2), ylo, 1], rb1.at[0], me.at(dy=1))
    b1m = mail.post(part.at[ho, pl.ds(2, 2), ylo, 1], rb1.at[1], me.at(dy=-1))
    a1p.wait_recv()
    add_into(part.at[0, xp, :, 0], ra1.at[0])
    a2p = mail.post(part.at[:, xp, :, 0], ra2.at[0], me.at(dx=1))
    a1m.wait_recv()
    add_into(part.at[1, xm, :, 0], ra1.at[1])
    a2m = mail.post(part.at[:, xm, :, 0], ra2.at[1], me.at(dx=-1))
    b1p.wait_recv()
    add_into(part.at[hp, pl.ds(0, 2), lo, 1], rb1.at[0])
    b2p = mail.post(part.at[hp, :, lo, 1], rb2.at[0], me.at(dy=1))
    b1m.wait_recv()
    add_into(part.at[hm, pl.ds(2, 2), lo, 1], rb1.at[1])
    b2m = mail.post(part.at[hm, :, lo, 1], rb2.at[1], me.at(dy=-1))
    a2p.wait_recv()
    a2m.wait_recv()
    add_into(part.at[:, x, :, 0], ra2.at[0], ra2.at[1])
    c1p = mail.post(part.at[ho, x, ylo, 0, pl.ds(0, 64)], rc1.at[0], me.at(dy=1))
    c1m = mail.post(part.at[ho, x, ylo, 0, pl.ds(64, 64)], rc1.at[1], me.at(dy=-1))
    b2p.wait_recv()
    b2m.wait_recv()
    add_into(part.at[yhi, :, ylo, 1], rb2.at[0], rb2.at[1])
    d1p = mail.post(part.at[yhi, xo, ylo, 1, pl.ds(0, 64)], rd1.at[0], me.at(dx=1))
    d1m = mail.post(part.at[yhi, xo, ylo, 1, pl.ds(64, 64)], rd1.at[1], me.at(dx=-1))
    c1p.wait_recv()
    add_into(part.at[hp, x, lo, 0, pl.ds(0, 64)], rc1.at[0])
    c2p = mail.post(part.at[hp, x, lo, 0], rc2.at[0], me.at(dy=1))
    c1m.wait_recv()
    add_into(part.at[hm, x, lo, 0, pl.ds(64, 64)], rc1.at[1])
    c2m = mail.post(part.at[hm, x, lo, 0], rc2.at[1], me.at(dy=-1))
    d1p.wait_recv()
    add_into(part.at[yhi, xp, ylo, 1, pl.ds(0, 64)], rd1.at[0])
    d2p = mail.post(part.at[yhi, xp, ylo, 1], rd2.at[0], me.at(dx=1))
    d1m.wait_recv()
    add_into(part.at[yhi, xm, ylo, 1, pl.ds(64, 64)], rd1.at[1])
    d2m = mail.post(part.at[yhi, xm, ylo, 1], rd2.at[1], me.at(dx=-1))

    def owned(h, copies, parts):
        for copy in copies:
            copy.wait_recv()
        total = part[yhi, x, ylo, h].astype(F32)
        for piece in parts:
            total = total + piece[...].astype(F32)
        result[yhi, me.z, h] = total.astype(BF)

    owned(0, (c2p, c2m), (rc2.at[0], rc2.at[1]))
    owned(1, (d2p, d2m), (rd2.at[0], rd2.at[1]))

    z = me.z
    kinds = (yhi, 1 - yhi)

    def spot(k, dz):
        return result.at[kinds[k], (z + dz + 8) % 8]

    def pass_on(k, dz, step):
        return mail.post(spot(k, dz), spot(k, dz), me.at(dz=step))

    up, down = [None, None], [None, None]
    up[0], down[0] = pass_on(0, 0, 1), pass_on(0, 0, -1)
    swap = mail.post(spot(0, 0), spot(0, 0), me.at(dy=2))
    swap.wait_recv()
    up[1], down[1] = pass_on(1, 0, 1), pass_on(1, 0, -1)
    last = []
    for hop in range(1, 4):
        for k in range(2):
            up[k].wait_recv()
            if hop < 3 or k == 0:
                up[k] = pass_on(k, -hop, 1)
            down[k].wait_recv()
            if hop < 3 or k == 1:
                down[k] = pass_on(k, hop, -1)
    up[0].wait_recv()
    down[1].wait_recv()
    mail.drain()


VMEM = pl.BlockSpec(memory_space=pltpu.VMEM)
SMEM = pl.BlockSpec(memory_space=pltpu.SMEM)
ANY = pl.BlockSpec(memory_space=pl.ANY)
LIMIT = 56 * 2**20


def gather_kernel(k_ref, v_ref, kbuf, vbuf, send, recv, local_sem):
    me = Place()
    greet([me.at(dx=1), me.at(dx=-1), me.at(dy=1), me.at(dy=-1), me.at(dc=1)])
    gather_phase(me, Mail(send, recv), k_ref, v_ref, kbuf, vbuf, local_sem)


def compute_kernel(q, do, kb, vb, span, seg, dq, terms, *scratch):
    compute_phase(lax.axis_index("ctx"), q, do, kb, vb, span, seg, dq, terms, *scratch)


def reduce_kernel(terms, result, send, recv, *scratch):
    me = Place()
    greet(
        [me.at(dx=1), me.at(dx=-1), me.at(dy=1), me.at(dy=-1), me.at(dc=1)]
        + [me.at(dy=2), me.at(dz=1), me.at(dz=-1)]
    )
    reduce_phase(me, Mail(send, recv), terms, *scratch, result)


def per_device(queries, keys, values, d_out, span_order, segments):
    keys = keys.reshape(8, 2, BLK, HD)
    values = values.reshape(8, 2, BLK, HD)
    kb, vb = pl.pallas_call(
        gather_kernel,
        out_shape=[jax.ShapeDtypeStruct((32, BLK, HD), BF)] * 2,
        in_specs=[ANY, ANY],
        out_specs=[VMEM, VMEM],
        scratch_shapes=[
            pltpu.SemaphoreType.DMA((32,)),
            pltpu.SemaphoreType.DMA((32,)),
            pltpu.SemaphoreType.DMA((2,)),
        ],
        compiler_params=pltpu.CompilerParams(
            collective_id=0, has_side_effects=True, vmem_limit_bytes=LIMIT
        ),
        name="gather",
    )(keys, values)
    dq, terms = pl.pallas_call(
        compute_kernel,
        out_shape=[
            jax.ShapeDtypeStruct((256, 512), BF),
            jax.ShapeDtypeStruct((2, 4, 2, 2, 2, BLK, HD), BF),
        ],
        in_specs=[VMEM, VMEM, VMEM, VMEM, SMEM, VMEM],
        out_specs=[VMEM, VMEM],
        scratch_shapes=[
            pltpu.SMEM((32,), jnp.int32),
            pltpu.VMEM((2, COLS, HD), BF),
            pltpu.VMEM((2, COLS, HD), BF),
            pltpu.VMEM((WIN * BLK, HD), BF),
            pltpu.VMEM((WIN * BLK, HD), BF),
            pltpu.VMEM((WIN * BLK, COLS), F32),
            pltpu.VMEM((WIN * BLK, COLS), F32),
            pltpu.VMEM((2, WIN + 1, BLK, COLS), BF),
            pltpu.VMEM((2, WIN + 1, BLK, COLS), BF),
        ],
        compiler_params=pltpu.CompilerParams(vmem_limit_bytes=LIMIT),
        name="attend",
    )(queries, d_out, kb, vb, span_order, segments.reshape(32, BLK))
    result = pl.pallas_call(
        reduce_kernel,
        out_shape=jax.ShapeDtypeStruct((2, 8, 2, BLK, HD), BF),
        in_specs=[VMEM],
        out_specs=VMEM,
        scratch_shapes=[
            pltpu.SemaphoreType.DMA((40,)),
            pltpu.SemaphoreType.DMA((40,)),
            pltpu.VMEM((2, 4, 2, 2, BLK, HD), BF),
            pltpu.VMEM((2, 4, 2, 2, BLK, HD), BF),
            pltpu.VMEM((2, 2, BLK, HD), BF),
            pltpu.VMEM((2, 2, 2, BLK, HD), BF),
            pltpu.VMEM((2, 2, BLK, HD), BF),
            pltpu.VMEM((2, 4, BLK, HD), BF),
            pltpu.VMEM((2, 64, HD), BF),
            pltpu.VMEM((2, BLK, HD), BF),
            pltpu.VMEM((2, 64, HD), BF),
            pltpu.VMEM((2, BLK, HD), BF),
        ],
        compiler_params=pltpu.CompilerParams(
            collective_id=1, has_side_effects=True, vmem_limit_bytes=LIMIT
        ),
        name="reduce",
    )(terms)
    result = result.reshape(2, 8, 256, HD).astype(F32)
    return (dq, result[0], result[1])


def solution(mesh):
    return jax.shard_map(
        per_device,
        mesh=mesh,
        in_specs=(
            P("ctx", "tp"),
            P(None, "ctx", None),
            P(None, "ctx", None),
            P("ctx", "tp"),
            P(),
            P(),
        ),
        out_specs=(P("ctx", "tp"), P(None, "ctx", None), P(None, "ctx", None)),
        check_vma=False,
    )
```

time: 468 us -> 86.9 us (0.19)
  waiting for transfers between devices: 154 us -> 0 us
  local copies, waits for them, and re-layouts: 123 us -> 2.76 us
  matrix products: 87.3 us -> 0 us
  Pallas kernels: 0 us -> 82.9 us
  other arithmetic: 68.2 us -> 0 us
  loops' own time: 17.1 us -> 0 us
  between operations: 14 us -> 0.65 us
    all_gather x3 -> x0, waiting for transfers between devices: 88.8 us -> none  [the longest x1 88.8 us: per_device(): lax.all_gather(mine[None].astype(jnp.bfloat16), 'tp', axis=0, tiled=True)]
    dot_general x56 -> x0, matrix products: 87.3 us -> none  [the longest x8 24 us: output_step(): jnp.einsum('hqk,kd->qhd', probs16, value_block, preferred_element_type=jn...]
    pallas_call x0 -> x3, Pallas kernels: none -> 82.9 us  [the longest x1 48.1 us: per_device(): pl.pallas_call(reduce_kernel, out_shape=jax.ShapeDtypeStruct((2, 8, 2, BL...]
    reduce_scatter x1 -> x0, waiting for transfers between devices: 65.4 us -> none  [per_device(): lax.psum_scatter(terms.astype(jnp.bfloat16), 'ctx', scatter_dimension=0,...]
    dynamic_slice x74 -> x0, local copies, waits for them, and re-layouts: 57.9 us -> none  [the longest x24 19.8 us: per_device(): lax.scan(stats_step, (start_max, start_sum), steps_idx)]
    gather x4 -> x0, local copies, waits for them, and re-layouts: 46.1 us -> none  [the longest x1 40.5 us: per_device(): key_seg = segments[key_pos]]
    add x11 -> x0, other arithmetic: 41.9 us -> none  [the longest x1 16.2 us: per_device(): key_pos = span_order[all_rows // span] * span + all_rows % span]
    another operation x3 -> x0, loops' own time: 17.1 us -> none  [the longest x1 5.75 us: per_device(): lax.scan(stats_step, (start_max, start_sum), steps_idx)]
  transfers between devices with their start and end apart: 4 -> 0, of which waited for: 2 -> 0; matrix products, arithmetic and copies ran while one was open for 31% -> 0% of each run, Pallas kernels for 0% -> 0%
where the time goes in v1:
time: 86.9 us; the launch traced here: 86.4 us
  Pallas kernels  82.9 us (95%)
  local copies, waits for them, and re-layouts  2.76 us (3%)
    pallas_call x1, Pallas kernels, per_device(): pl.pallas_call(reduce_kernel, out_shape=jax.ShapeDtypeStruct((2, 8, 2, BL...  48.1 us
    pallas_call x1, Pallas kernels, per_device(): pl.pallas_call(gather_kernel, out_shape=[jax.ShapeDtypeStruct((32, BLK, H...  17.6 us
    pallas_call x1, Pallas kernels, per_device(): pl.pallas_call(compute_kernel, out_shape=[jax.ShapeDtypeStruct((256, 512)...  17.3 us
    slice x1, local copies, waits for them, and re-layouts, per_device(): return (dq, result[0], result[1])  2.76 us

profile of v1, /device:TPU:8, one launch (start us, length us, event | category | flops | bytes accessed | tf_op | source)
XLA Modules:
  0.0 86.4 jit_solution(15553794555779320399)
XLA Ops:
  0.6 17.6 %gather.1 = (bf16[32,128,128]{2,1,0:T(8,128)(2,1)}, bf16[32,128,128]{2,1,0:T(8,128)(2,1)}) custom-call(bf16[8,2,128,128]{3,2,1,0:T(8,128)(2,1)} %bitcast.7, bf16[8,2,128,128]{3,2,1,0:T(8,128)(2,1)} %bitcast.8), custom_call_target="tpu_custom_call" | custom-call | tf_op jit(solution)/shard_map/gather/pallas_call | solution.py:375
  18.3 17.3 %attend.1 = (bf16[256,512]{1,0:T(8,128)(2,1)}, bf16[2,4,2,2,2,128,128]{6,5,4,3,2,1,0:T(8,128)(2,1)}) custom-call(bf16[256,512]{1,0:T(8,128)(2,1)} %q.1, bf16[256,512]{1,0:T(8,128)(2,1)} %do.1, bf16[32,128,128]{2,1,0:T(8,128)(2,1)} %get-tuple-element.7.kb, bf16[32,128,128]{2,1,0:T(8,128)(2,1)} %get-tuple-element.8.vb, s32[32]{0:T(128)} %span.1, s32[32,128]{1,0:T(8,128)} %bitcast.9), custom_call_target="tpu_custom_call" | custom-call | tf_op jit(solution)/shard_map/attend/pallas_call | solution.py:390
  35.5 48.1 %reduce.1 = bf16[2,8,2,128,128]{4,3,2,1,0:T(8,128)(2,1)} custom-call(bf16[2,4,2,2,2,128,128]{6,5,4,3,2,1,0:T(8,128)(2,1)} %get-tuple-element.10.terms), custom_call_target="tpu_custom_call" | custom-call | tf_op jit(solution)/shard_map/reduce/pallas_call | solution.py:412
  83.6 2.8 %fusion = (f32[1,8,2,128,128]{4,3,2,1,0:T(8,128)}, f32[1,8,2,128,128]{4,3,2,1,0:T(8,128)}) fusion(bf16[2,8,2,128,128]{4,3,2,1,0:T(8,128)(2,1)} %reduce.1), kind=kLoop, calls=%fused_computation | loop fusion | bytes 4194304 | tf_op jit(solution)/shard_map/slice | solution.py:437

commit v2 on v1

v2 whole, which is shorter than its diff:
```python
import functools

import jax
import jax.numpy as jnp
from jax import lax
from jax.experimental import pallas as pl
from jax.experimental.pallas import tpu as pltpu
from jax.sharding import PartitionSpec as P

HD = 128
BLK = 128
HEADS_DEV = 4
COLS = HEADS_DEV * BLK
WIN = 17
NEGATIVE = -1e30
SCALE = HD**-0.5
LOG2E = 1.4426950408889634
BF = jnp.bfloat16
F32 = jnp.float32


class Place:
    def __init__(self):
        self.ctx = lax.axis_index("ctx")
        self.tp = lax.axis_index("tp")
        self.x = self.ctx // 4
        self.ylo = (self.ctx // 2) % 2
        self.core = self.ctx % 2
        self.z = self.tp // 2
        self.yhi = self.tp % 2
        self.y = self.yhi * 2 + self.ylo

    def at(self, dx=0, dy=0, dc=0, dz=0):
        x = (self.x + dx + 4) % 4
        y = (self.y + dy + 4) % 4
        c = (self.core + dc) % 2
        z = (self.z + dz + 8) % 8
        return (x * 4 + (y % 2) * 2 + c, z * 2 + y // 2)

    def block(self, dx=0, dy=0, dc=0):
        return ((self.x + dx + 4) % 4) * 4 + ((self.ylo + dy) % 2) * 2 + (self.core + dc) % 2


class Mail:
    def __init__(self, send, recv):
        self.send, self.recv, self.used, self.out = send, recv, 0, []

    def post(self, src, dst, device):
        copy = pltpu.make_async_remote_copy(
            src_ref=src,
            dst_ref=dst,
            send_sem=self.send.at[self.used],
            recv_sem=self.recv.at[self.used],
            device_id=device,
            device_id_type=pl.DeviceIdType.MESH,
        )
        self.used += 1
        copy.start()
        self.out.append(copy)
        return copy

    def drain(self):
        for copy in self.out:
            copy.wait_send()
        self.out = []


def greet(devices):
    barrier = pltpu.get_barrier_semaphore()
    for device in devices:
        pl.semaphore_signal(
            barrier, inc=1, device_id=device, device_id_type=pl.DeviceIdType.MESH
        )
    pl.semaphore_wait(barrier, len(devices))


def gather_phase(me, mail, k_ref, v_ref, kbuf, vbuf, local_sem, meanwhile):
    own = me.block()
    src = (k_ref.at[me.z], v_ref.at[me.z])
    buf = (kbuf, vbuf)

    def at(kind, block):
        return buf[kind].at[pl.ds(2 * block, 2)]

    def forward(kind, block, device):
        return mail.post(at(kind, block), at(kind, block), device)

    local = []
    for kind in range(2):
        copy = pltpu.make_async_copy(src[kind], at(kind, own), local_sem.at[kind])
        copy.start()
        local.append(copy)
    ydir = (1, -1)
    xp, xm, y0, s0 = [], [], [], []
    for kind in range(2):
        xp.append(mail.post(src[kind], at(kind, own), me.at(dx=1)))
        xm.append(mail.post(src[kind], at(kind, own), me.at(dx=-1)))
        y0.append(mail.post(src[kind], at(kind, own), me.at(dy=ydir[kind])))
    for kind in range(2):
        s0.append(mail.post(src[kind], at(kind, own), me.at(dc=1)))
    meanwhile()
    x2, sib, yfar = [None, None], [], []
    for kind in range(2):
        xp[kind].wait_recv()
        block = me.block(dx=-1)
        if kind == 0:
            x2[0] = forward(0, block, me.at(dx=1))
        yfar.append((kind, -1, forward(kind, block, me.at(dy=ydir[kind]))))
        sib.append(forward(kind, block, me.at(dc=1)))
        xm[kind].wait_recv()
        block = me.block(dx=1)
        if kind == 1:
            x2[1] = forward(1, block, me.at(dx=-1))
        yfar.append((kind, 1, forward(kind, block, me.at(dy=ydir[kind]))))
        sib.append(forward(kind, block, me.at(dc=1)))
    for kind in range(2):
        y0[kind].wait_recv()
        sib.append(forward(kind, me.block(dy=1), me.at(dc=1)))
    for kind in range(2):
        x2[kind].wait_recv()
        block = me.block(dx=2)
        yfar.append((kind, 2, forward(kind, block, me.at(dy=ydir[kind]))))
        sib.append(forward(kind, block, me.at(dc=1)))
    for kind, dx, copy in yfar:
        copy.wait_recv()
        sib.append(forward(kind, me.block(dx=dx, dy=1), me.at(dc=1)))
    for copy in local:
        copy.wait()
    for copy in s0 + sib:
        copy.wait_recv()


CHUNKS = ((0, 6), (6, 12), (12, 17))


def prepare(span_ref, seg_ref, q_ref, do_ref, inv, qs, ds_rows, p_scr, ds_scr):
    for j in range(32):
        found = jnp.int32(0)
        for s in range(32):
            found = jnp.where(span_ref[s] == j, s, found)
        inv[j] = found
    zero = jnp.zeros((BLK, COLS), BF)
    for u in range(2):
        p_scr[u, WIN] = zero
        ds_scr[u, WIN] = zero
        for h in range(HEADS_DEV):
            qs[u, pl.ds(h * BLK, BLK), :] = q_ref[pl.ds(u * BLK, BLK), pl.ds(h * HD, HD)]
            ds_rows[u, pl.ds(h * BLK, BLK), :] = do_ref[pl.ds(u * BLK, BLK), pl.ds(h * HD, HD)]


def attend(
    ctx, kbuf, vbuf, span_ref, seg_ref, inv, qs, ds_rows, kg, vg, s_scr, dp_scr, p_scr, ds_scr
):
    seg_all = seg_ref[...]
    counts = [jnp.sum(jnp.where(seg_all == v, 1.0, 0.0)) for v in range(3)]
    c2 = SCALE * LOG2E
    cols2 = lax.broadcasted_iota(jnp.int32, (BLK, 2 * BLK), 1) % BLK
    rows2 = lax.broadcasted_iota(jnp.int32, (BLK, 2 * BLK), 0)
    causal = rows2 <= cols2
    rows_f = rows2.astype(F32)
    for u in range(2):
        p = span_ref[2 * ctx + u]
        for t in range(WIN):
            j = jnp.maximum(p - (WIN - 1) + t, 0)
            s = inv[j]
            kg[u, pl.ds(t * BLK, BLK), :] = kbuf[s]
            vg[pl.ds(t * BLK, BLK), :] = vbuf[s]
        seg_row = seg_ref[pl.ds(p, 1), :]
        start = jnp.zeros((1, BLK), F32)
        for v in range(3):
            start = start + jnp.where(seg_row > v, counts[v], 0.0)
        first = (p - (WIN - 1)) * BLK
        start = start - first.astype(F32)
        start2 = jnp.concatenate([start, start], axis=1)

        for hp in range(2):
            wide = pl.ds(hp * 256, 256)
            q2 = qs[u, wide, :]
            do2 = ds_rows[u, wide, :]
            top = jnp.full((8, 256), NEGATIVE, F32)
            for t0, t1 in CHUNKS:
                rows = pl.ds(t0 * BLK, (t1 - t0) * BLK)
                sc = lax.dot_general(
                    kg[u, rows, :], q2, (((1,), (1,)), ((), ())), preferred_element_type=F32
                )
                for t in range(t0, t1):
                    tile = sc[(t - t0) * BLK : (t - t0 + 1) * BLK]
                    ok = rows_f >= start2 - float(t * BLK)
                    if t == WIN - 1:
                        ok = ok & causal
                    tile = jnp.where(ok, tile * c2, NEGATIVE)
                    s_scr[pl.ds(t * BLK, BLK), wide] = tile
                    top = jnp.maximum(top, jnp.max(tile.reshape(16, 8, 256), axis=0))
            top = jnp.max(top, axis=0, keepdims=True)
            norm = jnp.zeros((8, 256), F32)
            mixed = jnp.zeros((8, 256), F32)
            for t0, t1 in CHUNKS:
                rows = pl.ds(t0 * BLK, (t1 - t0) * BLK)
                dp = lax.dot_general(
                    vg[rows, :], do2, (((1,), (1,)), ((), ())), preferred_element_type=F32
                )
                for t in range(t0, t1):
                    tile = pl.ds(t * BLK, BLK)
                    dpt = dp[(t - t0) * BLK : (t - t0 + 1) * BLK]
                    pt = jnp.exp2(s_scr[tile, wide] - top)
                    s_scr[tile, wide] = pt
                    dp_scr[tile, wide] = dpt
                    norm = norm + jnp.sum(pt.reshape(16, 8, 256), axis=0)
                    mixed = mixed + jnp.sum((pt * dpt).reshape(16, 8, 256), axis=0)
            inv_norm = 1.0 / jnp.sum(norm, axis=0, keepdims=True)
            delta = jnp.sum(mixed, axis=0, keepdims=True) * inv_norm
            for t in range(WIN):
                tile = pl.ds(t * BLK, BLK)
                prob = s_scr[tile, wide] * inv_norm
                p_scr[u, t, :, wide] = prob.astype(BF)
                ds_scr[u, t, :, wide] = (prob * (dp_scr[tile, wide] - delta)).astype(BF)


def query_grads(dq_ref, kg, ds_scr):
    for u in range(2):
        for hp in range(2):
            wide = pl.ds(hp * 256, 256)
            dqt = jnp.zeros((HD, 256), F32)
            for t0, t1 in CHUNKS:
                dsc = ds_scr[u, pl.ds(t0, t1 - t0), :, wide].reshape((t1 - t0) * BLK, 256)
                dqt = dqt + lax.dot_general(
                    kg[u, pl.ds(t0 * BLK, (t1 - t0) * BLK), :], dsc,
                    (((0,), (0,)), ((), ())), preferred_element_type=F32,
                )
            for i in range(2):
                piece = (dqt[:, i * BLK : (i + 1) * BLK] * SCALE).T
                dq_ref[pl.ds(u * BLK, BLK), pl.ds((2 * hp + i) * HD, HD)] = piece.astype(BF)


def key_terms(ctx, span_ref, kind, core, source, weights, terms):
    base = [span_ref[2 * ctx + u] - (WIN - 1) for u in range(2)]

    @pl.loop(0, 2)
    def _(xx):
        picks = []
        for i in range(8):
            x2, lo, h = i // 4, (i // 2) % 2, i % 2
            where = span_ref[(xx * 2 + x2) * 8 + lo * 4 + core * 2 + h]
            pick = []
            for u in range(2):
                t = where - base[u]
                pick.append(jnp.where((t >= 0) & (t < WIN), t, WIN))
            picks.append(pick)
        total = None
        for u in range(2):
            left = jnp.concatenate([source[u, picks[i][u]] for i in range(8)], axis=0)
            part = jnp.dot(left, weights[u], preferred_element_type=F32)
            total = part if total is None else total + part
        if kind == 0:
            total = total * SCALE
        terms[pl.ds(xx * 2, 2)] = total.astype(BF).reshape(2, 2, 2, BLK, HD)


class Stream:
    def __init__(self, me, mail, kind, theirs, mine, r0, a1, b1, a2, b2, result):
        self.me, self.mail, self.kind = me, mail, kind
        self.theirs, self.mine, self.r0 = theirs, mine, r0
        self.a1, self.b1, self.a2, self.b2 = a1, b1, a2, b2
        self.result = result

    def to_sibling(self):
        self.half = self.mail.post(self.theirs, self.r0, self.me.at(dc=1))

    def first_leg(self):
        me, mine = self.me, self.mine
        self.half.wait_recv()
        for xx in range(4):
            mine[xx] = (mine[xx].astype(F32) + self.r0[xx].astype(F32)).astype(BF)
        self.leg1 = []
        for i, d in enumerate((1, -1, 2)):
            x = (me.x + d + 4) % 4
            y = (me.y + d + 4) % 4
            self.leg1.append(
                self.mail.post(mine.at[x, :, :, pl.ds(0, 64)], self.a1.at[i], me.at(dx=d))
            )
            self.leg1.append(
                self.mail.post(mine.at[:, y % 2, y // 2, pl.ds(64, 64)], self.b1.at[i], me.at(dy=d))
            )

    def second_leg(self):
        me, mine = self.me, self.mine
        for copy in self.leg1:
            copy.wait_recv()
        own_a = mine.at[me.x, :, :, pl.ds(0, 64)]
        own_b = mine.at[:, me.ylo, me.yhi, pl.ds(64, 64)]
        for own, got in ((own_a, self.a1), (own_b, self.b1)):
            total = own[...].astype(F32)
            for i in range(3):
                total = total + got[i].astype(F32)
            own[...] = total.astype(BF)
        self.leg2 = []
        for i, d in enumerate((1, -1, 2)):
            x = (me.x + d + 4) % 4
            y = (me.y + d + 4) % 4
            self.leg2.append(
                self.mail.post(
                    mine.at[me.x, y % 2, y // 2, pl.ds(0, 64)], self.a2.at[i], me.at(dy=d)
                )
            )
            self.leg2.append(
                self.mail.post(
                    mine.at[x, me.ylo, me.yhi, pl.ds(64, 64)], self.b2.at[i], me.at(dx=d)
                )
            )

    def spot(self, k, dz):
        half = self.me.yhi if k == 0 else 1 - self.me.yhi
        return self.result.at[self.kind, (self.me.z + dz + 8) % 8, half]

    def pass_on(self, k, dz, step):
        return self.mail.post(self.spot(k, dz), self.spot(k, dz), self.me.at(dz=step))

    def finish(self):
        me, mine = self.me, self.mine
        for copy in self.leg2:
            copy.wait_recv()
        own = self.spot(0, 0)
        for rows, got in ((pl.ds(0, 64), self.a2), (pl.ds(64, 64), self.b2)):
            total = mine[me.x, me.ylo, me.yhi, rows].astype(F32)
            for i in range(3):
                total = total + got[i].astype(F32)
            self.result[self.kind, me.z, me.yhi, rows] = total.astype(BF)
        self.up, self.down = [None, None], [None, None]
        self.up[0], self.down[0] = self.pass_on(0, 0, 1), self.pass_on(0, 0, -1)
        self.swap = self.mail.post(own, own, me.at(dy=2))

    def swapped(self):
        self.swap.wait_recv()
        self.up[1], self.down[1] = self.pass_on(1, 0, 1), self.pass_on(1, 0, -1)

    def hop(self, hop, k):
        self.up[k].wait_recv()
        if hop < 3 or (hop == 3 and k == 0):
            self.up[k] = self.pass_on(k, -hop, 1)
        self.down[k].wait_recv()
        if hop < 3 or (hop == 3 and k == 1):
            self.down[k] = self.pass_on(k, hop, -1)

    def last(self):
        self.up[0].wait_recv()
        self.down[1].wait_recv()


VMEM = pl.BlockSpec(memory_space=pltpu.VMEM)
SMEM = pl.BlockSpec(memory_space=pltpu.SMEM)
ANY = pl.BlockSpec(memory_space=pl.ANY)
LIMIT = 56 * 2**20


def kernel(
    q_ref, k_ref, v_ref, do_ref, span_ref, seg_ref, dq_ref, result,
    send, recv, local_sem, kbuf, vbuf, inv, qs, ds_rows, kg, vg, s_scr, dp_scr, p_scr, ds_scr,
    theirs, mine, r0, a1, b1, a2, b2,
):
    me = Place()
    greet(
        [me.at(dx=1), me.at(dx=-1), me.at(dx=2), me.at(dy=1), me.at(dy=-1), me.at(dy=2)]
        + [me.at(dc=1), me.at(dz=1), me.at(dz=-1)]
    )
    mail = Mail(send, recv)
    gather_phase(
        me, mail, k_ref, v_ref, kbuf, vbuf, local_sem,
        lambda: prepare(span_ref, seg_ref, q_ref, do_ref, inv, qs, ds_rows, p_scr, ds_scr),
    )
    attend(
        me.ctx, kbuf, vbuf, span_ref, seg_ref, inv, qs, ds_rows, kg, vg, s_scr, dp_scr,
        p_scr, ds_scr,
    )
    dk, dv = (
        Stream(
            me, mail, kind, theirs.at[kind], mine.at[kind], r0.at[kind], a1.at[kind],
            b1.at[kind], a2.at[kind], b2.at[kind], result,
        )
        for kind in range(2)
    )
    work = {0: (ds_scr, qs), 1: (p_scr, ds_rows)}

    def terms(stream, core, out):
        key_terms(me.ctx, span_ref, stream.kind, core, *work[stream.kind], out)

    terms(dv, 1 - me.core, dv.theirs)
    dv.to_sibling()
    terms(dv, me.core, dv.mine)
    dv.first_leg()
    terms(dk, 1 - me.core, dk.theirs)
    dk.to_sibling()
    terms(dk, me.core, dk.mine)
    dk.first_leg()
    dv.second_leg()
    query_grads(dq_ref, kg, ds_scr)
    dv.finish()
    dk.second_leg()
    dv.swapped()
    dv.hop(1, 0)
    dk.finish()
    dv.hop(1, 1)
    dk.swapped()
    dv.hop(2, 0)
    dv.hop(2, 1)
    dk.hop(1, 0)
    dk.hop(1, 1)
    dv.hop(3, 0)
    dv.hop(3, 1)
    dk.hop(2, 0)
    dk.hop(2, 1)
    dv.last()
    dk.hop(3, 0)
    dk.hop(3, 1)
    dk.last()
    mail.drain()


def per_device(queries, keys, values, d_out, span_order, segments):
    keys = keys.reshape(8, 2, BLK, HD)
    values = values.reshape(8, 2, BLK, HD)
    dq, result = pl.pallas_call(
        kernel,
        out_shape=[
            jax.ShapeDtypeStruct((256, 512), BF),
            jax.ShapeDtypeStruct((2, 8, 2, BLK, HD), BF),
        ],
        in_specs=[VMEM, ANY, ANY, VMEM, SMEM, VMEM],
        out_specs=[VMEM, VMEM],
        scratch_shapes=[
            pltpu.SemaphoreType.DMA((96,)),
            pltpu.SemaphoreType.DMA((96,)),
            pltpu.SemaphoreType.DMA((2,)),
            pltpu.VMEM((32, BLK, HD), BF),
            pltpu.VMEM((32, BLK, HD), BF),
            pltpu.SMEM((32,), jnp.int32),
            pltpu.VMEM((2, COLS, HD), BF),
            pltpu.VMEM((2, COLS, HD), BF),
            pltpu.VMEM((2, WIN * BLK, HD), BF),
            pltpu.VMEM((WIN * BLK, HD), BF),
            pltpu.VMEM((WIN * BLK, COLS), F32),
            pltpu.VMEM((WIN * BLK, COLS), F32),
            pltpu.VMEM((2, WIN + 1, BLK, COLS), BF),
            pltpu.VMEM((2, WIN + 1, BLK, COLS), BF),
            pltpu.VMEM((2, 4, 2, 2, BLK, HD), BF),
            pltpu.VMEM((2, 4, 2, 2, BLK, HD), BF),
            pltpu.VMEM((2, 4, 2, 2, BLK, HD), BF),
            pltpu.VMEM((2, 3, 2, 2, 64, HD), BF),
            pltpu.VMEM((2, 3, 4, 64, HD), BF),
            pltpu.VMEM((2, 3, 64, HD), BF),
            pltpu.VMEM((2, 3, 64, HD), BF),
        ],
        compiler_params=pltpu.CompilerParams(
            collective_id=0, has_side_effects=True, vmem_limit_bytes=LIMIT
        ),
        name="backward",
    )(queries, keys, values, d_out, span_order, segments.reshape(32, BLK))
    result = result.reshape(2, 8, 256, HD).astype(F32)
    return (dq, result[0], result[1])


def solution(mesh):
    return jax.shard_map(
        per_device,
        mesh=mesh,
        in_specs=(
            P("ctx", "tp"),
            P(None, "ctx", None),
            P(None, "ctx", None),
            P("ctx", "tp"),
            P(),
            P(),
        ),
        out_specs=(P("ctx", "tp"), P(None, "ctx", None), P(None, "ctx", None)),
        check_vma=False,
    )
```

time: 86.9 us -> 69.7 us (0.80)
  Pallas kernels: 82.9 us -> 65.4 us
    pallas_call x3 -> x1, Pallas kernels: 82.9 us -> 65.4 us  [per_device(): pl.pallas_call(kernel, out_shape=[jax.ShapeDtypeStruct((256, 512), BF), j...]
where the time goes in v2:
time: 69.7 us; the launch traced here: 69.5 us
  Pallas kernels  65.4 us (94%)
  local copies, waits for them, and re-layouts  3.51 us (5%)
    pallas_call x1, Pallas kernels, per_device(): pl.pallas_call(kernel, out_shape=[jax.ShapeDtypeStruct((256, 512), BF), j...  65.4 us
    slice x1, local copies, waits for them, and re-layouts, per_device(): return (dq, result[0], result[1])  2.8 us

profile of v2, /device:TPU:8, one launch (start us, length us, event | category | flops | bytes accessed | tf_op | source)
XLA Modules:
  0.0 69.5 jit_solution(2315149683544279238)
XLA Ops:
  0.6 65.4 %backward.1 = (bf16[256,512]{1,0:T(8,128)(2,1)}, bf16[2,8,2,128,128]{4,3,2,1,0:T(8,128)(2,1)}) custom-call(bf16[256,512]{1,0:T(8,128)(2,1)} %q_ref.1, bf16[8,2,128,128]{3,2,1,0:T(8,128)(2,1)} %bitcast.7, bf16[8,2,128,128]{3,2,1,0:T(8,128)(2,1)} %bitcast.8, bf16[256,512]{1,0:T(8,128)(2,1)} %do_ref.1, s32[32]{0:T(128)} %span_ref.1, s32[32,128]{1,0:T(8,128)} %bitcast.9), custom_call_target="tpu_custom_call" | custom-call | tf_op jit(solution)/shard_map/backward/pallas_call | solution.py:421
  66.0 0.0 copy-start
  66.0 2.8 %fusion = (f32[1,8,2,128,128]{4,3,2,1,0:T(8,128)}, f32[1,8,2,128,128]{4,3,2,1,0:T(8,128)}) fusion(bf16[2,8,2,128,128]{4,3,2,1,0:T(8,128)(2,1)} %get-tuple-element.6), kind=kLoop, calls=%fused_computation | loop fusion | bytes 4194304 | tf_op jit(solution)/shard_map/slice | solution.py:458
  68.8 0.0 copy-done
  68.8 0.7 %copy.10 = bf16[256,512]{1,0:T(8,128)(2,1)} copy(bf16[256,512]{1,0:T(8,128)(2,1)S(1)} %copy-done) | data formatting | bytes 524288
Async XLA Ops:
  66.0 2.8 %copy-start = (bf16[256,512]{1,0:T(8,128)(2,1)S(1)}, bf16[256,512]{1,0:T(8,128)(2,1)}, u32[]{:S(2)}) copy-start(bf16[256,512]{1,0:T(8,128)(2,1)} %get-tuple-element.12) | copy-start | bytes 786436

commit v3 on v2

v3 whole, which is shorter than its diff:
```python
import functools

import jax
import jax.numpy as jnp
from jax import lax
from jax.experimental import pallas as pl
from jax.experimental.pallas import tpu as pltpu
from jax.sharding import PartitionSpec as P

HD = 128
BLK = 128
HEADS_DEV = 4
COLS = HEADS_DEV * BLK
WIN = 17
NEGATIVE = -1e30
SCALE = HD**-0.5
LOG2E = 1.4426950408889634
BF = jnp.bfloat16
F32 = jnp.float32


class Place:
    def __init__(self):
        self.ctx = lax.axis_index("ctx")
        self.tp = lax.axis_index("tp")
        self.x = self.ctx // 4
        self.ylo = (self.ctx // 2) % 2
        self.core = self.ctx % 2
        self.z = self.tp // 2
        self.yhi = self.tp % 2
        self.y = self.yhi * 2 + self.ylo

    def at(self, dx=0, dy=0, dc=0, dz=0):
        x = (self.x + dx + 4) % 4
        y = (self.y + dy + 4) % 4
        c = (self.core + dc) % 2
        z = (self.z + dz + 8) % 8
        return (x * 4 + (y % 2) * 2 + c, z * 2 + y // 2)

    def block(self, dx=0, dy=0, dc=0):
        return ((self.x + dx + 4) % 4) * 4 + ((self.ylo + dy) % 2) * 2 + (self.core + dc) % 2


class Mail:
    def __init__(self, send, recv):
        self.send, self.recv, self.used, self.out = send, recv, 0, []

    def post(self, src, dst, device):
        copy = pltpu.make_async_remote_copy(
            src_ref=src,
            dst_ref=dst,
            send_sem=self.send.at[self.used],
            recv_sem=self.recv.at[self.used],
            device_id=device,
            device_id_type=pl.DeviceIdType.MESH,
        )
        self.used += 1
        copy.start()
        self.out.append(copy)
        return copy

    def drain(self):
        for copy in self.out:
            copy.wait_send()
        self.out = []


def greet(devices):
    barrier = pltpu.get_barrier_semaphore()
    for device in devices:
        pl.semaphore_signal(
            barrier, inc=1, device_id=device, device_id_type=pl.DeviceIdType.MESH
        )
    pl.semaphore_wait(barrier, len(devices))


class Gather:
    def __init__(self, me, mail, src, buf, local_sem):
        self.me, self.mail, self.src, self.buf, self.local_sem = me, mail, src, buf, local_sem
        self.sib, self.far = [], []

    def whole(self, block):
        return self.buf.at[pl.ds(2 * block, 2)]

    def half(self, block, h):
        return self.buf.at[2 * block + h]

    def share(self, block, h=None):
        ref = self.whole(block) if h is None else self.half(block, h)
        self.sib.append(self.mail.post(ref, ref, self.me.at(dc=1)))

    def along_y(self, dx, h):
        ref = self.half(self.me.block(dx=dx), h)
        copy = self.mail.post(ref, ref, self.me.at(dy=1 - 2 * h))
        self.far.append((dx, h, copy))

    def own_x(self):
        me, own = self.me, self.me.block()
        self.local = pltpu.make_async_copy(self.src, self.whole(own), self.local_sem)
        self.local.start()
        self.xs = [
            (-d, self.mail.post(self.src, self.whole(own), me.at(dx=d))) for d in (1, -1)
        ]

    def own_y(self):
        me, own = self.me, self.me.block()
        self.y0 = [
            self.mail.post(self.src.at[h], self.half(own, h), me.at(dy=1 - 2 * h))
            for h in range(2)
        ]
        self.sib.append(self.mail.post(self.src, self.whole(own), me.at(dc=1)))

    def from_x(self):
        self.x2 = []
        for h, (dx, copy) in enumerate(self.xs):
            copy.wait_recv()
            block = self.me.block(dx=dx)
            ref = self.half(block, h)
            self.x2.append(self.mail.post(ref, ref, self.me.at(dx=-dx)))
            for i in range(2):
                self.along_y(dx, i)
            self.share(block)

    def from_y(self):
        for h in range(2):
            self.y0[h].wait_recv()
        self.share(self.me.block(dy=1))

    def from_x2(self):
        for h in range(2):
            self.x2[h].wait_recv()
            self.along_y(2, h)
        self.share(self.me.block(dx=2))

    def from_far(self, first, last):
        for i in range(first, last):
            dx, h, copy = self.far[i]
            copy.wait_recv()
            if h == 1:
                self.share(self.me.block(dx=dx, dy=1))

    def complete(self):
        self.local.wait()
        for copy in self.sib:
            copy.wait_recv()


CHUNKS = ((0, 6), (6, 12), (12, 17))


def prepare(span_ref, q_ref, do_ref, inv, qs, ds_rows, w_scr):
    for j in range(32):
        found = jnp.int32(0)
        for s in range(32):
            found = jnp.where(span_ref[s] == j, s, found)
        inv[j] = found
    zero = jnp.zeros((BLK, HD), F32)
    for u in range(2):
        w_scr[u, WIN] = zero
        for h in range(HEADS_DEV):
            qs[u, pl.ds(h * BLK, BLK), :] = q_ref[pl.ds(u * BLK, BLK), pl.ds(h * HD, HD)]
            ds_rows[u, pl.ds(h * BLK, BLK), :] = do_ref[pl.ds(u * BLK, BLK), pl.ds(h * HD, HD)]


def window(ctx, u, span_ref, inv, buf, out):
    p = span_ref[2 * ctx + u]
    for t in range(WIN):
        out[u, pl.ds(t * BLK, BLK), :] = buf[inv[jnp.maximum(p - (WIN - 1) + t, 0)]]


def nt_dot(a, b):
    return lax.dot_general(a, b, (((1,), (1,)), ((), ())), preferred_element_type=F32)


def probs_of(ctx, u, span_ref, seg_ref, qs, kg, s_scr, p_scr):
    p = span_ref[2 * ctx + u]
    seg_all = seg_ref[...]
    counts = [jnp.sum(jnp.where(seg_all == v, 1.0, 0.0)) for v in range(3)]
    cols2 = lax.broadcasted_iota(jnp.int32, (BLK, 2 * BLK), 1) % BLK
    rows2 = lax.broadcasted_iota(jnp.int32, (BLK, 2 * BLK), 0)
    causal = rows2 <= cols2
    rows_f = rows2.astype(F32)
    seg_row = seg_ref[pl.ds(p, 1), :]
    start = jnp.zeros((1, BLK), F32)
    for v in range(3):
        start = start + jnp.where(seg_row > v, counts[v], 0.0)
    first = (p - (WIN - 1)) * BLK
    start = start - first.astype(F32)
    start2 = jnp.concatenate([start, start], axis=1)
    inv_norms = []
    for hp in range(2):
        wide = pl.ds(hp * 256, 256)
        q2 = qs[u, wide, :]
        top = jnp.full((8, 256), NEGATIVE, F32)
        for t0, t1 in CHUNKS:
            sc = nt_dot(kg[u, pl.ds(t0 * BLK, (t1 - t0) * BLK), :], q2)
            for t in range(t0, t1):
                tile = sc[(t - t0) * BLK : (t - t0 + 1) * BLK]
                ok = rows_f >= start2 - float(t * BLK)
                if t == WIN - 1:
                    ok = ok & causal
                tile = jnp.where(ok, tile * (SCALE * LOG2E), NEGATIVE)
                s_scr[u, pl.ds(t * BLK, BLK), wide] = tile
                top = jnp.maximum(top, jnp.max(tile.reshape(16, 8, 256), axis=0))
        top = jnp.max(top, axis=0, keepdims=True)
        norm = jnp.zeros((8, 256), F32)
        for t in range(WIN):
            tile = pl.ds(t * BLK, BLK)
            pt = jnp.exp2(s_scr[u, tile, wide] - top)
            s_scr[u, tile, wide] = pt
            norm = norm + jnp.sum(pt.reshape(16, 8, 256), axis=0)
        inv_norm = 1.0 / jnp.sum(norm, axis=0, keepdims=True)
        for t in range(WIN):
            tile = pl.ds(t * BLK, BLK)
            p_scr[u, tile, wide] = (s_scr[u, tile, wide] * inv_norm).astype(BF)
        inv_norms.append(inv_norm)
    return inv_norms


def dscores_of(u, inv_norms, ds_rows, vg, s_scr, dp_scr, ds_scr):
    for hp in range(2):
        wide = pl.ds(hp * 256, 256)
        do2 = ds_rows[u, wide, :]
        mixed = jnp.zeros((8, 256), F32)
        for t0, t1 in CHUNKS:
            dp = nt_dot(vg[u, pl.ds(t0 * BLK, (t1 - t0) * BLK), :], do2)
            for t in range(t0, t1):
                tile = pl.ds(t * BLK, BLK)
                dpt = dp[(t - t0) * BLK : (t - t0 + 1) * BLK]
                dp_scr[tile, wide] = dpt
                mixed = mixed + jnp.sum(
                    (s_scr[u, tile, wide] * dpt).reshape(16, 8, 256), axis=0
                )
        inv_norm = inv_norms[hp]
        delta = jnp.sum(mixed, axis=0, keepdims=True) * inv_norm
        for t in range(WIN):
            tile = pl.ds(t * BLK, BLK)
            prob = s_scr[u, tile, wide] * inv_norm
            ds_scr[u, tile, wide] = (prob * (dp_scr[tile, wide] - delta)).astype(BF)


def query_grads(dq_ref, kg, ds_scr):
    for u in range(2):
        for hp in range(2):
            dqt = lax.dot_general(
                kg[u], ds_scr[u, :, pl.ds(hp * 256, 256)],
                (((0,), (0,)), ((), ())), preferred_element_type=F32,
            )
            for i in range(2):
                piece = (dqt[:, i * BLK : (i + 1) * BLK] * SCALE).T
                dq_ref[pl.ds(u * BLK, BLK), pl.ds((2 * hp + i) * HD, HD)] = piece.astype(BF)


def window_terms(u, source, weights, w_scr):
    for t0, t1 in CHUNKS:
        part = jnp.dot(
            source[u, pl.ds(t0 * BLK, (t1 - t0) * BLK), :], weights[u], preferred_element_type=F32
        )
        w_scr[u, pl.ds(t0, t1 - t0)] = part.reshape(t1 - t0, BLK, HD)


def assemble(ctx, span_ref, kind, core, w_scr, terms):
    base = [span_ref[2 * ctx + u] - (WIN - 1) for u in range(2)]
    for i in range(16):
        xx, lo, h = i // 4, (i // 2) % 2, i % 2
        where = span_ref[xx * 8 + lo * 4 + core * 2 + h]
        total = None
        for u in range(2):
            t = where - base[u]
            piece = w_scr[u, jnp.where((t >= 0) & (t < WIN), t, WIN)]
            total = piece if total is None else total + piece
        if kind == 0:
            total = total * SCALE
        terms[xx, lo, h] = total.astype(BF)


class Stream:
    def __init__(self, me, mail, kind, theirs, mine, r0, a1, b1, a2, b2, result):
        self.me, self.mail, self.kind = me, mail, kind
        self.theirs, self.mine, self.r0 = theirs, mine, r0
        self.a1, self.b1, self.a2, self.b2 = a1, b1, a2, b2
        self.result = result

    def to_sibling(self):
        self.half = self.mail.post(self.theirs, self.r0, self.me.at(dc=1))

    def first_leg(self):
        me, mine = self.me, self.mine
        self.half.wait_recv()
        for xx in range(4):
            mine[xx] = (mine[xx].astype(F32) + self.r0[xx].astype(F32)).astype(BF)
        self.leg1 = []
        for i, d in enumerate((1, -1, 2)):
            x = (me.x + d + 4) % 4
            y = (me.y + d + 4) % 4
            self.leg1.append(
                self.mail.post(mine.at[x, :, :, pl.ds(0, 64)], self.a1.at[i], me.at(dx=d))
            )
            self.leg1.append(
                self.mail.post(mine.at[:, y % 2, y // 2, pl.ds(64, 64)], self.b1.at[i], me.at(dy=d))
            )

    def second_leg(self):
        me, mine = self.me, self.mine
        for copy in self.leg1:
            copy.wait_recv()
        own_a = mine.at[me.x, :, :, pl.ds(0, 64)]
        own_b = mine.at[:, me.ylo, me.yhi, pl.ds(64, 64)]
        for own, got in ((own_a, self.a1), (own_b, self.b1)):
            total = own[...].astype(F32)
            for i in range(3):
                total = total + got[i].astype(F32)
            own[...] = total.astype(BF)
        self.leg2 = []
        for i, d in enumerate((1, -1, 2)):
            x = (me.x + d + 4) % 4
            y = (me.y + d + 4) % 4
            self.leg2.append(
                self.mail.post(
                    mine.at[me.x, y % 2, y // 2, pl.ds(0, 64)], self.a2.at[i], me.at(dy=d)
                )
            )
            self.leg2.append(
                self.mail.post(
                    mine.at[x, me.ylo, me.yhi, pl.ds(64, 64)], self.b2.at[i], me.at(dx=d)
                )
            )

    def spot(self, k, dz):
        half = self.me.yhi if k == 0 else 1 - self.me.yhi
        return self.result.at[self.kind, (self.me.z + dz + 8) % 8, half]

    def pass_on(self, k, dz, step):
        return self.mail.post(self.spot(k, dz), self.spot(k, dz), self.me.at(dz=step))

    def over(self, dz):
        return self.mail.post(self.spot(0, dz), self.spot(0, dz), self.me.at(dy=2))

    def finish(self):
        me, mine = self.me, self.mine
        for copy in self.leg2:
            copy.wait_recv()
        for rows, got in ((pl.ds(0, 64), self.a2), (pl.ds(64, 64), self.b2)):
            total = mine[me.x, me.ylo, me.yhi, rows].astype(F32)
            for i in range(3):
                total = total + got[i].astype(F32)
            self.result[self.kind, me.z, me.yhi, rows] = total.astype(BF)
        self.up, self.down = [None, None], [None, None]
        self.up[0], self.down[0] = self.pass_on(0, 0, 1), self.pass_on(0, 0, -1)
        self.swaps = [self.over(0)]

    def swapped(self):
        self.swaps[0].wait_recv()
        self.up[1], self.down[1] = self.pass_on(1, 0, 1), self.pass_on(1, 0, -1)

    def hop(self, hop, k):
        self.up[k].wait_recv()
        if hop < (3, 2)[k] or (hop == 3 and self.kind == 0):
            self.up[k] = self.pass_on(k, -hop, 1)
        if hop == 3:
            self.swaps.append(self.over(-hop))
        self.down[k].wait_recv()
        if hop < (3, 2)[k] or (hop == 3 and self.kind == 1):
            self.down[k] = self.pass_on(k, hop, -1)
        if hop == 3:
            self.swaps.append(self.over(hop))

    def farthest(self):
        (self.up[0] if self.kind == 0 else self.down[0]).wait_recv()
        self.swaps.append(self.over(4))

    def last(self):
        for copy in self.swaps[1:]:
            copy.wait_recv()


VMEM = pl.BlockSpec(memory_space=pltpu.VMEM)
SMEM = pl.BlockSpec(memory_space=pltpu.SMEM)
ANY = pl.BlockSpec(memory_space=pl.ANY)
LIMIT = 56 * 2**20


def kernel(
    q_ref, k_ref, v_ref, do_ref, span_ref, seg_ref, dq_ref, result,
    send, recv, local_sem, kbuf, vbuf, inv, qs, ds_rows, kg, vg, s_scr, dp_scr, p_scr, ds_scr,
    w_scr, theirs, mine, r0, a1, b1, a2, b2,
):
    me = Place()
    greet(
        [me.at(dx=1), me.at(dx=-1), me.at(dx=2), me.at(dy=1), me.at(dy=-1), me.at(dy=2)]
        + [me.at(dc=1), me.at(dz=1), me.at(dz=-1)]
    )
    mail = Mail(send, recv)
    gk = Gather(me, mail, k_ref.at[me.z], kbuf, local_sem.at[0])
    gv = Gather(me, mail, v_ref.at[me.z], vbuf, local_sem.at[1])
    gk.own_x()
    gk.own_y()
    gv.own_x()
    prepare(span_ref, q_ref, do_ref, inv, qs, ds_rows, w_scr)
    gk.from_x()
    gv.own_y()
    gk.from_y()
    gv.from_x()
    gk.from_x2()
    gk.from_far(0, 4)
    gv.from_y()
    gv.from_x2()
    gk.from_far(4, 6)
    gk.complete()
    ctx = me.ctx
    window(ctx, 0, span_ref, inv, kbuf, kg)
    norms = [probs_of(ctx, 0, span_ref, seg_ref, qs, kg, s_scr, p_scr)]
    gv.from_far(0, 6)
    window_terms(0, p_scr, ds_rows, w_scr)
    window(ctx, 1, span_ref, inv, kbuf, kg)
    norms.append(probs_of(ctx, 1, span_ref, seg_ref, qs, kg, s_scr, p_scr))
    window_terms(1, p_scr, ds_rows, w_scr)
    dk, dv = (
        Stream(
            me, mail, kind, theirs.at[kind], mine.at[kind], r0.at[kind], a1.at[kind],
            b1.at[kind], a2.at[kind], b2.at[kind], result,
        )
        for kind in range(2)
    )
    assemble(ctx, span_ref, 1, 1 - me.core, w_scr, dv.theirs)
    dv.to_sibling()
    assemble(ctx, span_ref, 1, me.core, w_scr, dv.mine)
    gv.complete()
    window(ctx, 0, span_ref, inv, vbuf, vg)
    dscores_of(0, norms[0], ds_rows, vg, s_scr, dp_scr, ds_scr)
    dv.first_leg()
    window_terms(0, ds_scr, qs, w_scr)
    window(ctx, 1, span_ref, inv, vbuf, vg)
    dscores_of(1, norms[1], ds_rows, vg, s_scr, dp_scr, ds_scr)
    window_terms(1, ds_scr, qs, w_scr)
    assemble(ctx, span_ref, 0, 1 - me.core, w_scr, dk.theirs)
    dk.to_sibling()
    dv.second_leg()
    assemble(ctx, span_ref, 0, me.core, w_scr, dk.mine)
    query_grads(dq_ref, kg, ds_scr)
    dk.first_leg()
    dv.finish()
    dv.swapped()
    dk.second_leg()
    dv.hop(1, 0)
    dv.hop(1, 1)
    dk.finish()
    dv.hop(2, 0)
    dk.swapped()
    dv.hop(2, 1)
    dk.hop(1, 0)
    dv.hop(3, 0)
    dk.hop(1, 1)
    dk.hop(2, 0)
    dv.farthest()
    dk.hop(2, 1)
    dk.hop(3, 0)
    dk.farthest()
    dv.last()
    dk.last()
    mail.drain()


def per_device(queries, keys, values, d_out, span_order, segments):
    keys = keys.reshape(8, 2, BLK, HD)
    values = values.reshape(8, 2, BLK, HD)
    dq, result = pl.pallas_call(
        kernel,
        out_shape=[
            jax.ShapeDtypeStruct((256, 512), BF),
            jax.ShapeDtypeStruct((2, 8, 2, BLK, HD), BF),
        ],
        in_specs=[VMEM, ANY, ANY, VMEM, SMEM, VMEM],
        out_specs=[VMEM, VMEM],
        scratch_shapes=[
            pltpu.SemaphoreType.DMA((112,)),
            pltpu.SemaphoreType.DMA((112,)),
            pltpu.SemaphoreType.DMA((2,)),
            pltpu.VMEM((32, BLK, HD), BF),
            pltpu.VMEM((32, BLK, HD), BF),
            pltpu.SMEM((32,), jnp.int32),
            pltpu.VMEM((2, COLS, HD), BF),
            pltpu.VMEM((2, COLS, HD), BF),
            pltpu.VMEM((2, WIN * BLK, HD), BF),
            pltpu.VMEM((2, WIN * BLK, HD), BF),
            pltpu.VMEM((2, WIN * BLK, COLS), F32),
            pltpu.VMEM((WIN * BLK, COLS), F32),
            pltpu.VMEM((2, WIN * BLK, COLS), BF),
            pltpu.VMEM((2, WIN * BLK, COLS), BF),
            pltpu.VMEM((2, WIN + 1, BLK, HD), F32),
            pltpu.VMEM((2, 4, 2, 2, BLK, HD), BF),
            pltpu.VMEM((2, 4, 2, 2, BLK, HD), BF),
            pltpu.VMEM((2, 4, 2, 2, BLK, HD), BF),
            pltpu.VMEM((2, 3, 2, 2, 64, HD), BF),
            pltpu.VMEM((2, 3, 4, 64, HD), BF),
            pltpu.VMEM((2, 3, 64, HD), BF),
            pltpu.VMEM((2, 3, 64, HD), BF),
        ],
        compiler_params=pltpu.CompilerParams(
            collective_id=0, has_side_effects=True, vmem_limit_bytes=LIMIT
        ),
        name="backward",
    )(queries, keys, values, d_out, span_order, segments.reshape(32, BLK))
    result = result.reshape(2, 8, 256, HD).astype(F32)
    return (dq, result[0], result[1])


def solution(mesh):
    return jax.shard_map(
        per_device,
        mesh=mesh,
        in_specs=(
            P("ctx", "tp"),
            P(None, "ctx", None),
            P(None, "ctx", None),
            P("ctx", "tp"),
            P(),
            P(),
        ),
        out_specs=(P("ctx", "tp"), P(None, "ctx", None), P(None, "ctx", None)),
        check_vma=False,
    )
```

time: 69.7 us -> 70.7 us (1.014)
  Pallas kernels: 65.4 us -> 66.3 us
    pallas_call x1, Pallas kernels: 65.4 us -> 66.3 us  [per_device(): pl.pallas_call(kernel, out_shape=[jax.ShapeDtypeStruct((256, 512), BF), j...]
where the time goes in v3:
time: 70.7 us; the launch traced here: 70.4 us
  Pallas kernels  66.3 us (94%)
  local copies, waits for them, and re-layouts  3.51 us (5%)
    pallas_call x1, Pallas kernels, per_device(): pl.pallas_call(kernel, out_shape=[jax.ShapeDtypeStruct((256, 512), BF), j...  66.3 us
    slice x1, local copies, waits for them, and re-layouts, per_device(): return (dq, result[0], result[1])  2.8 us

profile of v3, /device:TPU:8, one launch (start us, length us, event | category | flops | bytes accessed | tf_op | source)
XLA Modules:
  0.0 70.4 jit_solution(10031322727808412996)
XLA Ops:
  0.6 66.3 %backward.1 = (bf16[256,512]{1,0:T(8,128)(2,1)}, bf16[2,8,2,128,128]{4,3,2,1,0:T(8,128)(2,1)}) custom-call(bf16[256,512]{1,0:T(8,128)(2,1)} %q_ref.1, bf16[8,2,128,128]{3,2,1,0:T(8,128)(2,1)} %bitcast.7, bf16[8,2,128,128]{3,2,1,0:T(8,128)(2,1)} %bitcast.8, bf16[256,512]{1,0:T(8,128)(2,1)} %do_ref.1, s32[32]{0:T(128)} %span_ref.1, s32[32,128]{1,0:T(8,128)} %bitcast.9), custom_call_target="tpu_custom_call" | custom-call | tf_op jit(solution)/shard_map/backward/pallas_call | solution.py:467
  66.9 0.0 copy-start
  66.9 2.8 %fusion = (f32[1,8,2,128,128]{4,3,2,1,0:T(8,128)}, f32[1,8,2,128,128]{4,3,2,1,0:T(8,128)}) fusion(bf16[2,8,2,128,128]{4,3,2,1,0:T(8,128)(2,1)} %get-tuple-element.6), kind=kLoop, calls=%fused_computation | loop fusion | bytes 4194304 | tf_op jit(solution)/shard_map/slice | solution.py:505
  69.7 0.0 copy-done
  69.7 0.7 copy.10
Async XLA Ops:
  66.9 2.8 %copy-start = (bf16[256,512]{1,0:T(8,128)(2,1)S(1)}, bf16[256,512]{1,0:T(8,128)(2,1)}, u32[]{:S(2)}) copy-start(bf16[256,512]{1,0:T(8,128)(2,1)} %get-tuple-element.12) | copy-start | bytes 786436

commit v4 on v3

--- a/solution.py
+++ b/solution.py
@@ -99,7 +99,7 @@
         self.local = pltpu.make_async_copy(self.src, self.whole(own), self.local_sem)
         self.local.start()
         self.xs = [
-            (-d, self.mail.post(self.src, self.whole(own), me.at(dx=d))) for d in (1, -1)
+            (-d, self.mail.post(self.src, self.whole(own), me.at(dx=d))) for d in (1, -1, 2)
         ]
 
     def own_y(self):
@@ -110,27 +110,17 @@
         ]
         self.sib.append(self.mail.post(self.src, self.whole(own), me.at(dc=1)))
 
-    def from_x(self):
-        self.x2 = []
-        for h, (dx, copy) in enumerate(self.xs):
-            copy.wait_recv()
-            block = self.me.block(dx=dx)
-            ref = self.half(block, h)
-            self.x2.append(self.mail.post(ref, ref, self.me.at(dx=-dx)))
-            for i in range(2):
-                self.along_y(dx, i)
-            self.share(block)
+    def from_x(self, i):
+        dx, copy = self.xs[i]
+        copy.wait_recv()
+        for h in range(2):
+            self.along_y(dx, h)
+        self.share(self.me.block(dx=dx))
 
     def from_y(self):
         for h in range(2):
             self.y0[h].wait_recv()
         self.share(self.me.block(dy=1))
-
-    def from_x2(self):
-        for h in range(2):
-            self.x2[h].wait_recv()
-            self.along_y(2, h)
-        self.share(self.me.block(dx=2))
 
     def from_far(self, first, last):
         for i in range(first, last):
@@ -330,9 +320,6 @@
         half = self.me.yhi if k == 0 else 1 - self.me.yhi
         return self.result.at[self.kind, (self.me.z + dz + 8) % 8, half]
 
-    def pass_on(self, k, dz, step):
-        return self.mail.post(self.spot(k, dz), self.spot(k, dz), self.me.at(dz=step))
-
     def over(self, dz):
         return self.mail.post(self.spot(0, dz), self.spot(0, dz), self.me.at(dy=2))
 
@@ -345,32 +332,19 @@
             for i in range(3):
                 total = total + got[i].astype(F32)
             self.result[self.kind, me.z, me.yhi, rows] = total.astype(BF)
-        self.up, self.down = [None, None], [None, None]
-        self.up[0], self.down[0] = self.pass_on(0, 0, 1), self.pass_on(0, 0, -1)
         self.swaps = [self.over(0)]
-
-    def swapped(self):
-        self.swaps[0].wait_recv()
-        self.up[1], self.down[1] = self.pass_on(1, 0, 1), self.pass_on(1, 0, -1)
-
-    def hop(self, hop, k):
-        self.up[k].wait_recv()
-        if hop < (3, 2)[k] or (hop == 3 and self.kind == 0):
-            self.up[k] = self.pass_on(k, -hop, 1)
-        if hop == 3:
-            self.swaps.append(self.over(-hop))
-        self.down[k].wait_recv()
-        if hop < (3, 2)[k] or (hop == 3 and self.kind == 1):
-            self.down[k] = self.pass_on(k, hop, -1)
-        if hop == 3:
-            self.swaps.append(self.over(hop))
-
-    def farthest(self):
-        (self.up[0] if self.kind == 0 else self.down[0]).wait_recv()
-        self.swaps.append(self.over(4))
+        self.direct = [
+            (-dz, self.mail.post(self.spot(0, 0), self.spot(0, 0), me.at(dz=dz)))
+            for dz in (1, -1, 2, -2, 3, -3, 4)
+        ]
+
+    def spread(self):
+        for dz, copy in self.direct:
+            copy.wait_recv()
+            self.swaps.append(self.over(dz))
 
     def last(self):
-        for copy in self.swaps[1:]:
+        for copy in self.swaps:
             copy.wait_recv()
 
 
@@ -388,7 +362,8 @@
     me = Place()
     greet(
         [me.at(dx=1), me.at(dx=-1), me.at(dx=2), me.at(dy=1), me.at(dy=-1), me.at(dy=2)]
-        + [me.at(dc=1), me.at(dz=1), me.at(dz=-1)]
+        + [me.at(dc=1)]
+        + [me.at(dz=dz) for dz in (1, -1, 2, -2, 3, -3, 4)]
     )
     mail = Mail(send, recv)
     gk = Gather(me, mail, k_ref.at[me.z], kbuf, local_sem.at[0])
@@ -397,14 +372,16 @@
     gk.own_y()
     gv.own_x()
     prepare(span_ref, q_ref, do_ref, inv, qs, ds_rows, w_scr)
-    gk.from_x()
+    gk.from_x(0)
+    gk.from_x(1)
     gv.own_y()
     gk.from_y()
-    gv.from_x()
-    gk.from_x2()
+    gk.from_x(2)
+    gv.from_x(0)
+    gv.from_x(1)
     gk.from_far(0, 4)
     gv.from_y()
-    gv.from_x2()
+    gv.from_x(2)
     gk.from_far(4, 6)
     gk.complete()
     ctx = me.ctx
@@ -435,27 +412,15 @@
     window_terms(1, ds_scr, qs, w_scr)
     assemble(ctx, span_ref, 0, 1 - me.core, w_scr, dk.theirs)
     dk.to_sibling()
+    assemble(ctx, span_ref, 0, me.core, w_scr, dk.mine)
     dv.second_leg()
-    assemble(ctx, span_ref, 0, me.core, w_scr, dk.mine)
+    dk.first_leg()
     query_grads(dq_ref, kg, ds_scr)
-    dk.first_leg()
     dv.finish()
-    dv.swapped()
     dk.second_leg()
-    dv.hop(1, 0)
-    dv.hop(1, 1)
+    dv.spread()
     dk.finish()
-    dv.hop(2, 0)
-    dk.swapped()
-    dv.hop(2, 1)
-    dk.hop(1, 0)
-    dv.hop(3, 0)
-    dk.hop(1, 1)
-    dk.hop(2, 0)
-    dv.farthest()
-    dk.hop(2, 1)
-    dk.hop(3, 0)
-    dk.farthest()
+    dk.spread()
     dv.last()
     dk.last()
     mail.drain()

time: 70.7 us -> 64.5 us (0.912)
  Pallas kernels: 66.3 us -> 60 us
    pallas_call x1, Pallas kernels: 66.3 us -> 60 us  [per_device(): pl.pallas_call(kernel, out_shape=[jax.ShapeDtypeStruct((256, 512), BF), j...]
where the time goes in v4:
time: 64.5 us; the launch traced here: 64.2 us
  Pallas kernels  60 us (93%)
  local copies, waits for them, and re-layouts  3.51 us (5%)
  between operations  0.65 us (1%)
    pallas_call x1, Pallas kernels, per_device(): pl.pallas_call(kernel, out_shape=[jax.ShapeDtypeStruct((256, 512), BF), j...  60 us
    slice x1, local copies, waits for them, and re-layouts, per_device(): return (dq, result[0], result[1])  2.8 us

profile of v4, /device:TPU:8, one launch (start us, length us, event | category | flops | bytes accessed | tf_op | source)
XLA Modules:
  0.0 64.2 jit_solution(11929597816171655874)
XLA Ops:
  0.6 60.0 %backward.1 = (bf16[256,512]{1,0:T(8,128)(2,1)}, bf16[2,8,2,128,128]{4,3,2,1,0:T(8,128)(2,1)}) custom-call(bf16[256,512]{1,0:T(8,128)(2,1)} %q_ref.1, bf16[8,2,128,128]{3,2,1,0:T(8,128)(2,1)} %bitcast.7, bf16[8,2,128,128]{3,2,1,0:T(8,128)(2,1)} %bitcast.8, bf16[256,512]{1,0:T(8,128)(2,1)} %do_ref.1, s32[32]{0:T(128)} %span_ref.1, s32[32,128]{1,0:T(8,128)} %bitcast.9), custom_call_target="tpu_custom_call" | custom-call | tf_op jit(solution)/shard_map/backward/pallas_call | solution.py:432
  60.7 0.0 copy-start
  60.7 2.8 %fusion = (f32[1,8,2,128,128]{4,3,2,1,0:T(8,128)}, f32[1,8,2,128,128]{4,3,2,1,0:T(8,128)}) fusion(bf16[2,8,2,128,128]{4,3,2,1,0:T(8,128)(2,1)} %get-tuple-element.6), kind=kLoop, calls=%fused_computation | loop fusion | bytes 4194304 | tf_op jit(solution)/shard_map/slice | solution.py:470
  63.5 0.0 copy-done
  63.5 0.7 %copy.10 = bf16[256,512]{1,0:T(8,128)(2,1)} copy(bf16[256,512]{1,0:T(8,128)(2,1)S(1)} %copy-done) | data formatting | bytes 524288
Async XLA Ops:
  60.7 2.8 %copy-start = (bf16[256,512]{1,0:T(8,128)(2,1)S(1)}, bf16[256,512]{1,0:T(8,128)(2,1)}, u32[]{:S(2)}) copy-start(bf16[256,512]{1,0:T(8,128)(2,1)} %get-tuple-element.12) | copy-start | bytes 786436

commit v5 on v4

--- a/solution.py
+++ b/solution.py
@@ -138,7 +138,7 @@
 CHUNKS = ((0, 6), (6, 12), (12, 17))
 
 
-def prepare(span_ref, q_ref, do_ref, inv, qs, ds_rows, w_scr):
+def prepare(span_ref, inv, w_scr):
     for j in range(32):
         found = jnp.int32(0)
         for s in range(32):
@@ -147,6 +147,10 @@
     zero = jnp.zeros((BLK, HD), F32)
     for u in range(2):
         w_scr[u, WIN] = zero
+
+
+def stack_heads(q_ref, do_ref, qs, ds_rows):
+    for u in range(2):
         for h in range(HEADS_DEV):
             qs[u, pl.ds(h * BLK, BLK), :] = q_ref[pl.ds(u * BLK, BLK), pl.ds(h * HD, HD)]
             ds_rows[u, pl.ds(h * BLK, BLK), :] = do_ref[pl.ds(u * BLK, BLK), pl.ds(h * HD, HD)]
@@ -162,7 +166,7 @@
     return lax.dot_general(a, b, (((1,), (1,)), ((), ())), preferred_element_type=F32)
 
 
-def probs_of(ctx, u, span_ref, seg_ref, qs, kg, s_scr, p_scr):
+def probs_of(ctx, u, span_ref, seg_ref, qs, ds_rows, qn, dn, kg, s_scr, p_scr):
     p = span_ref[2 * ctx + u]
     seg_all = seg_ref[...]
     counts = [jnp.sum(jnp.where(seg_all == v, 1.0, 0.0)) for v in range(3)]
@@ -198,11 +202,15 @@
             tile = pl.ds(t * BLK, BLK)
             pt = jnp.exp2(s_scr[u, tile, wide] - top)
             s_scr[u, tile, wide] = pt
+            p_scr[u, tile, wide] = pt.astype(BF)
             norm = norm + jnp.sum(pt.reshape(16, 8, 256), axis=0)
         inv_norm = 1.0 / jnp.sum(norm, axis=0, keepdims=True)
-        for t in range(WIN):
-            tile = pl.ds(t * BLK, BLK)
-            p_scr[u, tile, wide] = (s_scr[u, tile, wide] * inv_norm).astype(BF)
+        for i in range(2):
+            row = inv_norm[:, i * BLK : (i + 1) * BLK]
+            by_row = jnp.broadcast_to(row, (BLK, BLK)).T
+            part = pl.ds((2 * hp + i) * BLK, BLK)
+            qn[u, part, :] = (qs[u, part, :].astype(F32) * by_row).astype(BF)
+            dn[u, part, :] = (ds_rows[u, part, :].astype(F32) * by_row).astype(BF)
         inv_norms.append(inv_norm)
     return inv_norms
 
@@ -221,23 +229,21 @@
                 mixed = mixed + jnp.sum(
                     (s_scr[u, tile, wide] * dpt).reshape(16, 8, 256), axis=0
                 )
-        inv_norm = inv_norms[hp]
-        delta = jnp.sum(mixed, axis=0, keepdims=True) * inv_norm
+        delta = jnp.sum(mixed, axis=0, keepdims=True) * inv_norms[hp]
         for t in range(WIN):
             tile = pl.ds(t * BLK, BLK)
-            prob = s_scr[u, tile, wide] * inv_norm
-            ds_scr[u, tile, wide] = (prob * (dp_scr[tile, wide] - delta)).astype(BF)
-
-
-def query_grads(dq_ref, kg, ds_scr):
+            ds_scr[u, tile, wide] = (s_scr[u, tile, wide] * (dp_scr[tile, wide] - delta)).astype(BF)
+
+
+def query_grads(dq_ref, kg, ds_scr, norms):
     for u in range(2):
         for hp in range(2):
             dqt = lax.dot_general(
                 kg[u], ds_scr[u, :, pl.ds(hp * 256, 256)],
                 (((0,), (0,)), ((), ())), preferred_element_type=F32,
-            )
+            ) * (norms[u][hp] * SCALE)
             for i in range(2):
-                piece = (dqt[:, i * BLK : (i + 1) * BLK] * SCALE).T
+                piece = dqt[:, i * BLK : (i + 1) * BLK].T
                 dq_ref[pl.ds(u * BLK, BLK), pl.ds((2 * hp + i) * HD, HD)] = piece.astype(BF)
 
 
@@ -265,11 +271,11 @@
 
 
 class Stream:
-    def __init__(self, me, mail, kind, theirs, mine, r0, a1, b1, a2, b2, result):
+    def __init__(self, me, mail, kind, theirs, mine, r0, a1, b1, a2, b2, own, sem, result):
         self.me, self.mail, self.kind = me, mail, kind
         self.theirs, self.mine, self.r0 = theirs, mine, r0
         self.a1, self.b1, self.a2, self.b2 = a1, b1, a2, b2
-        self.result = result
+        self.own, self.sem, self.result = own, sem, result
 
     def to_sibling(self):
         self.half = self.mail.post(self.theirs, self.r0, self.me.at(dc=1))
@@ -331,10 +337,12 @@
             total = mine[me.x, me.ylo, me.yhi, rows].astype(F32)
             for i in range(3):
                 total = total + got[i].astype(F32)
-            self.result[self.kind, me.z, me.yhi, rows] = total.astype(BF)
-        self.swaps = [self.over(0)]
+            self.own[rows] = total.astype(BF)
+        self.kept = pltpu.make_async_copy(self.own, self.spot(0, 0), self.sem)
+        self.kept.start()
+        self.swaps = [self.mail.post(self.own, self.spot(0, 0), me.at(dy=2))]
         self.direct = [
-            (-dz, self.mail.post(self.spot(0, 0), self.spot(0, 0), me.at(dz=dz)))
+            (-dz, self.mail.post(self.own, self.spot(0, 0), me.at(dz=dz)))
             for dz in (1, -1, 2, -2, 3, -3, 4)
         ]
 
@@ -344,6 +352,7 @@
             self.swaps.append(self.over(dz))
 
     def last(self):
+        self.kept.wait()
         for copy in self.swaps:
             copy.wait_recv()
 
@@ -356,8 +365,8 @@
 
 def kernel(
     q_ref, k_ref, v_ref, do_ref, span_ref, seg_ref, dq_ref, result,
-    send, recv, local_sem, kbuf, vbuf, inv, qs, ds_rows, kg, vg, s_scr, dp_scr, p_scr, ds_scr,
-    w_scr, theirs, mine, r0, a1, b1, a2, b2,
+    send, recv, local_sem, q_rows, do_rows, dq_rows, kbuf, vbuf, inv, qs, ds_rows, qn, dn, kg, vg,
+    s_scr, dp_scr, p_scr, ds_scr, w_scr, theirs, mine, r0, a1, b1, a2, b2, own,
 ):
     me = Place()
     greet(
@@ -371,7 +380,16 @@
     gk.own_x()
     gk.own_y()
     gv.own_x()
-    prepare(span_ref, q_ref, do_ref, inv, qs, ds_rows, w_scr)
+    loads = [
+        pltpu.make_async_copy(q_ref, q_rows, local_sem.at[2]),
+        pltpu.make_async_copy(do_ref, do_rows, local_sem.at[3]),
+    ]
+    for load in loads:
+        load.start()
+    prepare(span_ref, inv, w_scr)
+    for load in loads:
+        load.wait()
+    stack_heads(q_rows, do_rows, qs, ds_rows)
     gk.from_x(0)
     gk.from_x(1)
     gv.own_y()
@@ -386,16 +404,16 @@
     gk.complete()
     ctx = me.ctx
     window(ctx, 0, span_ref, inv, kbuf, kg)
-    norms = [probs_of(ctx, 0, span_ref, seg_ref, qs, kg, s_scr, p_scr)]
+    norms = [probs_of(ctx, 0, span_ref, seg_ref, qs, ds_rows, qn, dn, kg, s_scr, p_scr)]
     gv.from_far(0, 6)
-    window_terms(0, p_scr, ds_rows, w_scr)
+    window_terms(0, p_scr, dn, w_scr)
     window(ctx, 1, span_ref, inv, kbuf, kg)
-    norms.append(probs_of(ctx, 1, span_ref, seg_ref, qs, kg, s_scr, p_scr))
-    window_terms(1, p_scr, ds_rows, w_scr)
+    norms.append(probs_of(ctx, 1, span_ref, seg_ref, qs, ds_rows, qn, dn, kg, s_scr, p_scr))
+    window_terms(1, p_scr, dn, w_scr)
     dk, dv = (
         Stream(
             me, mail, kind, theirs.at[kind], mine.at[kind], r0.at[kind], a1.at[kind],
-            b1.at[kind], a2.at[kind], b2.at[kind], result,
+            b1.at[kind], a2.at[kind], b2.at[kind], own.at[kind], local_sem.at[4 + kind], result,
         )
         for kind in range(2)
     )
@@ -406,16 +424,18 @@
     window(ctx, 0, span_ref, inv, vbuf, vg)
     dscores_of(0, norms[0], ds_rows, vg, s_scr, dp_scr, ds_scr)
     dv.first_leg()
-    window_terms(0, ds_scr, qs, w_scr)
+    window_terms(0, ds_scr, qn, w_scr)
     window(ctx, 1, span_ref, inv, vbuf, vg)
     dscores_of(1, norms[1], ds_rows, vg, s_scr, dp_scr, ds_scr)
-    window_terms(1, ds_scr, qs, w_scr)
+    window_terms(1, ds_scr, qn, w_scr)
     assemble(ctx, span_ref, 0, 1 - me.core, w_scr, dk.theirs)
     dk.to_sibling()
     assemble(ctx, span_ref, 0, me.core, w_scr, dk.mine)
     dv.second_leg()
     dk.first_leg()
-    query_grads(dq_ref, kg, ds_scr)
+    query_grads(dq_rows, kg, ds_scr, norms)
+    leave = pltpu.make_async_copy(dq_rows, dq_ref, local_sem.at[6])
+    leave.start()
     dv.finish()
     dk.second_leg()
     dv.spread()
@@ -423,7 +443,32 @@
     dk.spread()
     dv.last()
     dk.last()
+    leave.wait()
     mail.drain()
+
+
+def cast_kernel(result, dq_in, dk, dv, dq_out, narrow, wide, sem_in, sem_out):
+    through = pltpu.make_async_copy(dq_in, dq_out, sem_out.at[8])
+    through.start()
+    outs = (dk, dv)
+    loads, stores = [], []
+    for i in range(8):
+        part = pl.ds(2 * (i % 4), 2)
+        copy = pltpu.make_async_copy(
+            result.at[i // 4, part], narrow.at[i // 4, part], sem_in.at[i]
+        )
+        copy.start()
+        loads.append(copy)
+    for i in range(8):
+        part = pl.ds(2 * (i % 4), 2)
+        loads[i].wait()
+        wide[i // 4, part] = narrow[i // 4, part].astype(F32)
+        copy = pltpu.make_async_copy(wide.at[i // 4, part], outs[i // 4].at[part], sem_out.at[i])
+        copy.start()
+        stores.append(copy)
+    for copy in stores:
+        copy.wait()
+    through.wait()
 
 
 def per_device(queries, keys, values, d_out, span_order, segments):
@@ -435,15 +480,20 @@
             jax.ShapeDtypeStruct((256, 512), BF),
             jax.ShapeDtypeStruct((2, 8, 2, BLK, HD), BF),
         ],
-        in_specs=[VMEM, ANY, ANY, VMEM, SMEM, VMEM],
-        out_specs=[VMEM, VMEM],
+        in_specs=[ANY, ANY, ANY, ANY, SMEM, VMEM],
+        out_specs=[ANY, ANY],
         scratch_shapes=[
             pltpu.SemaphoreType.DMA((112,)),
             pltpu.SemaphoreType.DMA((112,)),
-            pltpu.SemaphoreType.DMA((2,)),
+            pltpu.SemaphoreType.DMA((7,)),
+            pltpu.VMEM((256, 512), BF),
+            pltpu.VMEM((256, 512), BF),
+            pltpu.VMEM((256, 512), BF),
             pltpu.VMEM((32, BLK, HD), BF),
             pltpu.VMEM((32, BLK, HD), BF),
             pltpu.SMEM((32,), jnp.int32),
+            pltpu.VMEM((2, COLS, HD), BF),
+            pltpu.VMEM((2, COLS, HD), BF),
             pltpu.VMEM((2, COLS, HD), BF),
             pltpu.VMEM((2, COLS, HD), BF),
             pltpu.VMEM((2, WIN * BLK, HD), BF),
@@ -460,14 +510,32 @@
             pltpu.VMEM((2, 3, 4, 64, HD), BF),
             pltpu.VMEM((2, 3, 64, HD), BF),
             pltpu.VMEM((2, 3, 64, HD), BF),
+            pltpu.VMEM((2, BLK, HD), BF),
         ],
         compiler_params=pltpu.CompilerParams(
             collective_id=0, has_side_effects=True, vmem_limit_bytes=LIMIT
         ),
         name="backward",
     )(queries, keys, values, d_out, span_order, segments.reshape(32, BLK))
-    result = result.reshape(2, 8, 256, HD).astype(F32)
-    return (dq, result[0], result[1])
+    dk, dv, dq = pl.pallas_call(
+        cast_kernel,
+        out_shape=[
+            jax.ShapeDtypeStruct((8, 2, BLK, HD), F32),
+            jax.ShapeDtypeStruct((8, 2, BLK, HD), F32),
+            jax.ShapeDtypeStruct((256, 512), BF),
+        ],
+        in_specs=[ANY, ANY],
+        out_specs=[ANY, ANY, ANY],
+        scratch_shapes=[
+            pltpu.VMEM((2, 8, 2, BLK, HD), BF),
+            pltpu.VMEM((2, 8, 2, BLK, HD), F32),
+            pltpu.SemaphoreType.DMA((8,)),
+            pltpu.SemaphoreType.DMA((9,)),
+        ],
+        compiler_params=pltpu.CompilerParams(vmem_limit_bytes=LIMIT),
+        name="widen",
+    )(result, dq)
+    return (dq, dk.reshape(8, 256, HD), dv.reshape(8, 256, HD))
 
 
 def solution(mesh):

time: 64.5 us -> 69.5 us (1.078)
  Pallas kernels: 60 us -> 68.6 us
  local copies, waits for them, and re-layouts: 3.51 us -> 0 us
    pallas_call x0 -> x1, Pallas kernels: none -> 9.2 us  [per_device(): pl.pallas_call(cast_kernel, out_shape=[jax.ShapeDtypeStruct((8, 2, BLK, H...]
    slice x1 -> x0, local copies, waits for them, and re-layouts: 2.8 us -> none  [per_device(): return (dq, result[0], result[1])]
    unnamed x3 -> x0, local copies, waits for them, and re-layouts: 0.71 us -> none
where the time goes in v5:
time: 69.5 us; the launch traced here: 69.2 us
  Pallas kernels  68.6 us (99%)
    pallas_call x1, Pallas kernels, per_device(): pl.pallas_call(kernel, out_shape=[jax.ShapeDtypeStruct((256, 512), BF), j...  59.4 us
    pallas_call x1, Pallas kernels, per_device(): pl.pallas_call(cast_kernel, out_shape=[jax.ShapeDtypeStruct((8, 2, BLK, H...  9.2 us

profile of v5, /device:TPU:8, one launch (start us, length us, event | category | flops | bytes accessed | tf_op | source)
XLA Modules:
  0.0 69.2 jit_solution(16710909832898611923)
XLA Ops:
  0.6 59.4 %backward.1 = (bf16[256,512]{1,0:T(8,128)(2,1)}, bf16[2,8,2,128,128]{4,3,2,1,0:T(8,128)(2,1)}) custom-call(bf16[256,512]{1,0:T(8,128)(2,1)} %q_ref.1, bf16[8,2,128,128]{3,2,1,0:T(8,128)(2,1)} %bitcast.5, bf16[8,2,128,128]{3,2,1,0:T(8,128)(2,1)} %bitcast.6, bf16[256,512]{1,0:T(8,128)(2,1)} %do_ref.1, s32[32]{0:T(128)} %span_ref.1, s32[32,128]{1,0:T(8,128)} %bitcast.7), custom_call_target="tpu_custom_call" | custom-call | tf_op jit(solution)/shard_map/backward/pallas_call | solution.py:477
  60.0 9.2 %widen.1 = (f32[8,2,128,128]{3,2,1,0:T(8,128)}, f32[8,2,128,128]{3,2,1,0:T(8,128)}, bf16[256,512]{1,0:T(8,128)(2,1)}) custom-call(bf16[2,8,2,128,128]{4,3,2,1,0:T(8,128)(2,1)} %get-tuple-element.8.result, bf16[256,512]{1,0:T(8,128)(2,1)} %get-tuple-element.9.dq_in), custom_call_target="tpu_custom_call" | custom-call | tf_op jit(solution)/shard_map/widen/pallas_call | solution.py:520

commit v6 on v5

--- a/solution.py
+++ b/solution.py
@@ -447,9 +447,7 @@
     mail.drain()
 
 
-def cast_kernel(result, dq_in, dk, dv, dq_out, narrow, wide, sem_in, sem_out):
-    through = pltpu.make_async_copy(dq_in, dq_out, sem_out.at[8])
-    through.start()
+def cast_kernel(result, dq_in, dk, dv, dq_out, narrow, wide, passing, sem_in, sem_out):
     outs = (dk, dv)
     loads, stores = [], []
     for i in range(8):
@@ -459,6 +457,8 @@
         )
         copy.start()
         loads.append(copy)
+    inward = pltpu.make_async_copy(dq_in, passing, sem_in.at[8])
+    inward.start()
     for i in range(8):
         part = pl.ds(2 * (i % 4), 2)
         loads[i].wait()
@@ -466,9 +466,12 @@
         copy = pltpu.make_async_copy(wide.at[i // 4, part], outs[i // 4].at[part], sem_out.at[i])
         copy.start()
         stores.append(copy)
+    inward.wait()
+    outward = pltpu.make_async_copy(passing, dq_out, sem_out.at[8])
+    outward.start()
     for copy in stores:
         copy.wait()
-    through.wait()
+    outward.wait()
 
 
 def per_device(queries, keys, values, d_out, span_order, segments):
@@ -529,7 +532,8 @@
         scratch_shapes=[
             pltpu.VMEM((2, 8, 2, BLK, HD), BF),
             pltpu.VMEM((2, 8, 2, BLK, HD), F32),
-            pltpu.SemaphoreType.DMA((8,)),
+            pltpu.VMEM((256, 512), BF),
+            pltpu.SemaphoreType.DMA((9,)),
             pltpu.SemaphoreType.DMA((9,)),
         ],
         compiler_params=pltpu.CompilerParams(vmem_limit_bytes=LIMIT),

time: 69.5 us -> 62.7 us (0.902)
  Pallas kernels: 68.6 us -> 61.9 us
    pallas_call x1, Pallas kernels: 9.2 us -> 2.47 us  [per_device(): pl.pallas_call(cast_kernel, out_shape=[jax.ShapeDtypeStruct((8, 2, BLK, H...]
where the time goes in v6:
time: 62.7 us; the launch traced here: 62.5 us
  Pallas kernels  61.9 us (99%)
  between operations  0.64 us (1%)
    pallas_call x1, Pallas kernels, per_device(): pl.pallas_call(kernel, out_shape=[jax.ShapeDtypeStruct((256, 512), BF), j...  59.4 us
    pallas_call x1, Pallas kernels, per_device(): pl.pallas_call(cast_kernel, out_shape=[jax.ShapeDtypeStruct((8, 2, BLK, H...  2.47 us

profile of v6, /device:TPU:8, one launch (start us, length us, event | category | flops | bytes accessed | tf_op | source)
XLA Modules:
  0.0 62.5 jit_solution(9901464420104460612)
XLA Ops:
  0.6 59.4 %backward.1 = (bf16[256,512]{1,0:T(8,128)(2,1)}, bf16[2,8,2,128,128]{4,3,2,1,0:T(8,128)(2,1)}) custom-call(bf16[256,512]{1,0:T(8,128)(2,1)} %q_ref.1, bf16[8,2,128,128]{3,2,1,0:T(8,128)(2,1)} %bitcast.5, bf16[8,2,128,128]{3,2,1,0:T(8,128)(2,1)} %bitcast.6, bf16[256,512]{1,0:T(8,128)(2,1)} %do_ref.1, s32[32]{0:T(128)} %span_ref.1, s32[32,128]{1,0:T(8,128)} %bitcast.7), custom_call_target="tpu_custom_call" | custom-call | tf_op jit(solution)/shard_map/backward/pallas_call | solution.py:480
  60.0 2.5 %widen.1 = (f32[8,2,128,128]{3,2,1,0:T(8,128)}, f32[8,2,128,128]{3,2,1,0:T(8,128)}, bf16[256,512]{1,0:T(8,128)(2,1)}) custom-call(bf16[2,8,2,128,128]{4,3,2,1,0:T(8,128)(2,1)} %get-tuple-element.8.result, bf16[256,512]{1,0:T(8,128)(2,1)} %get-tuple-element.9.dq_in), custom_call_target="tpu_custom_call" | custom-call | tf_op jit(solution)/shard_map/widen/pallas_call | solution.py:523

commit v7 on v6

--- a/solution.py
+++ b/solution.py
@@ -343,17 +343,24 @@
         self.swaps = [self.mail.post(self.own, self.spot(0, 0), me.at(dy=2))]
         self.direct = [
             (-dz, self.mail.post(self.own, self.spot(0, 0), me.at(dz=dz)))
-            for dz in (1, -1, 2, -2, 3, -3, 4)
+            for dz in (4, 3, -3, 2, -2, 1, -1)
+        ]
+
+    def swapped(self):
+        self.swaps[0].wait_recv()
+        self.near = [
+            self.mail.post(self.spot(1, 0), self.spot(1, 0), self.me.at(dz=dz)) for dz in (1, -1)
         ]
 
     def spread(self):
         for dz, copy in self.direct:
             copy.wait_recv()
-            self.swaps.append(self.over(dz))
+            if abs(dz) != 1:
+                self.swaps.append(self.over(dz))
 
     def last(self):
         self.kept.wait()
-        for copy in self.swaps:
+        for copy in self.swaps[1:] + self.near:
             copy.wait_recv()
 
 
@@ -438,8 +445,10 @@
     leave.start()
     dv.finish()
     dk.second_leg()
+    dv.swapped()
+    dk.finish()
     dv.spread()
-    dk.finish()
+    dk.swapped()
     dk.spread()
     dv.last()
     dk.last()

time: 62.7 us -> 60.1 us (0.959)
  Pallas kernels: 61.9 us -> 59.3 us
    pallas_call x1, Pallas kernels: 59.4 us -> 56.8 us  [per_device(): pl.pallas_call(kernel, out_shape=[jax.ShapeDtypeStruct((256, 512), BF), j...]
where the time goes in v7:
time: 60.1 us; the launch traced here: 59.9 us
  Pallas kernels  59.3 us (99%)
  between operations  0.64 us (1%)
    pallas_call x1, Pallas kernels, per_device(): pl.pallas_call(kernel, out_shape=[jax.ShapeDtypeStruct((256, 512), BF), j...  56.8 us
    pallas_call x1, Pallas kernels, per_device(): pl.pallas_call(cast_kernel, out_shape=[jax.ShapeDtypeStruct((8, 2, BLK, H...  2.47 us

profile of v7, /device:TPU:8, one launch (start us, length us, event | category | flops | bytes accessed | tf_op | source)
XLA Modules:
  0.0 59.9 jit_solution(12618875148697080015)
XLA Ops:
  0.6 56.8 %backward.1 = (bf16[256,512]{1,0:T(8,128)(2,1)}, bf16[2,8,2,128,128]{4,3,2,1,0:T(8,128)(2,1)}) custom-call(bf16[256,512]{1,0:T(8,128)(2,1)} %q_ref.1, bf16[8,2,128,128]{3,2,1,0:T(8,128)(2,1)} %bitcast.5, bf16[8,2,128,128]{3,2,1,0:T(8,128)(2,1)} %bitcast.6, bf16[256,512]{1,0:T(8,128)(2,1)} %do_ref.1, s32[32]{0:T(128)} %span_ref.1, s32[32,128]{1,0:T(8,128)} %bitcast.7), custom_call_target="tpu_custom_call" | custom-call | tf_op jit(solution)/shard_map/backward/pallas_call | solution.py:489
  57.4 2.5 %widen.1 = (f32[8,2,128,128]{3,2,1,0:T(8,128)}, f32[8,2,128,128]{3,2,1,0:T(8,128)}, bf16[256,512]{1,0:T(8,128)(2,1)}) custom-call(bf16[2,8,2,128,128]{4,3,2,1,0:T(8,128)(2,1)} %get-tuple-element.8.result, bf16[256,512]{1,0:T(8,128)(2,1)} %get-tuple-element.9.dq_in), custom_call_target="tpu_custom_call" | custom-call | tf_op jit(solution)/shard_map/widen/pallas_call | solution.py:532

commit v8 on v7

--- a/solution.py
+++ b/solution.py
@@ -255,9 +255,9 @@
         w_scr[u, pl.ds(t0, t1 - t0)] = part.reshape(t1 - t0, BLK, HD)
 
 
-def assemble(ctx, span_ref, kind, core, w_scr, terms):
+def assemble(ctx, span_ref, kind, core, w_scr, terms, part):
     base = [span_ref[2 * ctx + u] - (WIN - 1) for u in range(2)]
-    for i in range(16):
+    for i in range(8 * part, 8 * part + 8):
         xx, lo, h = i // 4, (i // 2) % 2, i % 2
         where = span_ref[xx * 8 + lo * 4 + core * 2 + h]
         total = None
@@ -277,13 +277,16 @@
         self.a1, self.b1, self.a2, self.b2 = a1, b1, a2, b2
         self.own, self.sem, self.result = own, sem, result
 
-    def to_sibling(self):
-        self.half = self.mail.post(self.theirs, self.r0, self.me.at(dc=1))
+    def to_sibling(self, part):
+        xs = pl.ds(2 * part, 2)
+        copy = self.mail.post(self.theirs.at[xs], self.r0.at[xs], self.me.at(dc=1))
+        self.halves = [copy] if part == 0 else self.halves + [copy]
 
     def first_leg(self):
         me, mine = self.me, self.mine
-        self.half.wait_recv()
         for xx in range(4):
+            if xx % 2 == 0:
+                self.halves[xx // 2].wait_recv()
             mine[xx] = (mine[xx].astype(F32) + self.r0[xx].astype(F32)).astype(BF)
         self.leg1 = []
         for i, d in enumerate((1, -1, 2)):
@@ -393,10 +396,6 @@
     ]
     for load in loads:
         load.start()
-    prepare(span_ref, inv, w_scr)
-    for load in loads:
-        load.wait()
-    stack_heads(q_rows, do_rows, qs, ds_rows)
     gk.from_x(0)
     gk.from_x(1)
     gv.own_y()
@@ -404,9 +403,13 @@
     gk.from_x(2)
     gv.from_x(0)
     gv.from_x(1)
+    prepare(span_ref, inv, w_scr)
     gk.from_far(0, 4)
     gv.from_y()
     gv.from_x(2)
+    for load in loads:
+        load.wait()
+    stack_heads(q_rows, do_rows, qs, ds_rows)
     gk.from_far(4, 6)
     gk.complete()
     ctx = me.ctx
@@ -424,9 +427,11 @@
         )
         for kind in range(2)
     )
-    assemble(ctx, span_ref, 1, 1 - me.core, w_scr, dv.theirs)
-    dv.to_sibling()
-    assemble(ctx, span_ref, 1, me.core, w_scr, dv.mine)
+    for part in range(2):
+        assemble(ctx, span_ref, 1, 1 - me.core, w_scr, dv.theirs, part)
+        dv.to_sibling(part)
+    for part in range(2):
+        assemble(ctx, span_ref, 1, me.core, w_scr, dv.mine, part)
     gv.complete()
     window(ctx, 0, span_ref, inv, vbuf, vg)
     dscores_of(0, norms[0], ds_rows, vg, s_scr, dp_scr, ds_scr)
@@ -435,9 +440,11 @@
     window(ctx, 1, span_ref, inv, vbuf, vg)
     dscores_of(1, norms[1], ds_rows, vg, s_scr, dp_scr, ds_scr)
     window_terms(1, ds_scr, qn, w_scr)
-    assemble(ctx, span_ref, 0, 1 - me.core, w_scr, dk.theirs)
-    dk.to_sibling()
-    assemble(ctx, span_ref, 0, me.core, w_scr, dk.mine)
+    for part in range(2):
+        assemble(ctx, span_ref, 0, 1 - me.core, w_scr, dk.theirs, part)
+        dk.to_sibling(part)
+    for part in range(2):
+        assemble(ctx, span_ref, 0, me.core, w_scr, dk.mine, part)
     dv.second_leg()
     dk.first_leg()
     query_grads(dq_rows, kg, ds_scr, norms)

time: 60.1 us -> 60.4 us (level)
  no operation moved by 1% of the time
where the time goes in v8:
time: 60.4 us; the launch traced here: 59.6 us
  Pallas kernels  59 us (98%)
  between operations  0.64 us (1%)
    pallas_call x1, Pallas kernels, per_device(): pl.pallas_call(kernel, out_shape=[jax.ShapeDtypeStruct((256, 512), BF), j...  56.5 us
    pallas_call x1, Pallas kernels, per_device(): pl.pallas_call(cast_kernel, out_shape=[jax.ShapeDtypeStruct((8, 2, BLK, H...  2.47 us

profile of v8, /device:TPU:8, one launch (start us, length us, event | category | flops | bytes accessed | tf_op | source)
XLA Modules:
  0.0 59.6 jit_solution(17848161982221396377)
XLA Ops:
  0.6 56.5 %backward.1 = (bf16[256,512]{1,0:T(8,128)(2,1)}, bf16[2,8,2,128,128]{4,3,2,1,0:T(8,128)(2,1)}) custom-call(bf16[256,512]{1,0:T(8,128)(2,1)} %q_ref.1, bf16[8,2,128,128]{3,2,1,0:T(8,128)(2,1)} %bitcast.5, bf16[8,2,128,128]{3,2,1,0:T(8,128)(2,1)} %bitcast.6, bf16[256,512]{1,0:T(8,128)(2,1)} %do_ref.1, s32[32]{0:T(128)} %span_ref.1, s32[32,128]{1,0:T(8,128)} %bitcast.7), custom_call_target="tpu_custom_call" | custom-call | tf_op jit(solution)/shard_map/backward/pallas_call | solution.py:496
  57.2 2.5 %widen.1 = (f32[8,2,128,128]{3,2,1,0:T(8,128)}, f32[8,2,128,128]{3,2,1,0:T(8,128)}, bf16[256,512]{1,0:T(8,128)(2,1)}) custom-call(bf16[2,8,2,128,128]{4,3,2,1,0:T(8,128)(2,1)} %get-tuple-element.8.result, bf16[256,512]{1,0:T(8,128)(2,1)} %get-tuple-element.9.dq_in), custom_call_target="tpu_custom_call" | custom-call | tf_op jit(solution)/shard_map/widen/pallas_call | solution.py:539

commit v9 on v8

--- a/solution.py
+++ b/solution.py
@@ -99,7 +99,7 @@
         self.local = pltpu.make_async_copy(self.src, self.whole(own), self.local_sem)
         self.local.start()
         self.xs = [
-            (-d, self.mail.post(self.src, self.whole(own), me.at(dx=d))) for d in (1, -1, 2)
+            (-d, self.mail.post(self.src, self.whole(own), me.at(dx=d))) for d in (2, 1, -1)
         ]
 
     def own_y(self):
@@ -289,7 +289,7 @@
                 self.halves[xx // 2].wait_recv()
             mine[xx] = (mine[xx].astype(F32) + self.r0[xx].astype(F32)).astype(BF)
         self.leg1 = []
-        for i, d in enumerate((1, -1, 2)):
+        for i, d in enumerate((2, 1, -1)):
             x = (me.x + d + 4) % 4
             y = (me.y + d + 4) % 4
             self.leg1.append(
@@ -311,7 +311,7 @@
                 total = total + got[i].astype(F32)
             own[...] = total.astype(BF)
         self.leg2 = []
-        for i, d in enumerate((1, -1, 2)):
+        for i, d in enumerate((2, 1, -1)):
             x = (me.x + d + 4) % 4
             y = (me.y + d + 4) % 4
             self.leg2.append(

time: 60.4 us -> 61.4 us (1.017)
  Pallas kernels: 59 us -> 60.6 us
    pallas_call x1, Pallas kernels: 56.5 us -> 58.1 us  [per_device(): pl.pallas_call(kernel, out_shape=[jax.ShapeDtypeStruct((256, 512), BF), j...]
where the time goes in v9:
time: 61.4 us; the launch traced here: 61.2 us
  Pallas kernels  60.6 us (99%)
  between operations  0.64 us (1%)
    pallas_call x1, Pallas kernels, per_device(): pl.pallas_call(kernel, out_shape=[jax.ShapeDtypeStruct((256, 512), BF), j...  58.1 us
    pallas_call x1, Pallas kernels, per_device(): pl.pallas_call(cast_kernel, out_shape=[jax.ShapeDtypeStruct((8, 2, BLK, H...  2.47 us

profile of v9, /device:TPU:8, one launch (start us, length us, event | category | flops | bytes accessed | tf_op | source)
XLA Modules:
  0.0 61.2 jit_solution(12709068713595301314)
XLA Ops:
  0.6 58.1 %backward.1 = (bf16[256,512]{1,0:T(8,128)(2,1)}, bf16[2,8,2,128,128]{4,3,2,1,0:T(8,128)(2,1)}) custom-call(bf16[256,512]{1,0:T(8,128)(2,1)} %q_ref.1, bf16[8,2,128,128]{3,2,1,0:T(8,128)(2,1)} %bitcast.5, bf16[8,2,128,128]{3,2,1,0:T(8,128)(2,1)} %bitcast.6, bf16[256,512]{1,0:T(8,128)(2,1)} %do_ref.1, s32[32]{0:T(128)} %span_ref.1, s32[32,128]{1,0:T(8,128)} %bitcast.7), custom_call_target="tpu_custom_call" | custom-call | tf_op jit(solution)/shard_map/backward/pallas_call | solution.py:496
  58.7 2.5 %widen.1 = (f32[8,2,128,128]{3,2,1,0:T(8,128)}, f32[8,2,128,128]{3,2,1,0:T(8,128)}, bf16[256,512]{1,0:T(8,128)(2,1)}) custom-call(bf16[2,8,2,128,128]{4,3,2,1,0:T(8,128)(2,1)} %get-tuple-element.8.result, bf16[256,512]{1,0:T(8,128)(2,1)} %get-tuple-element.9.dq_in), custom_call_target="tpu_custom_call" | custom-call | tf_op jit(solution)/shard_map/widen/pallas_call | solution.py:539

commit v10 on v8

--- a/solution.py
+++ b/solution.py
@@ -201,7 +201,6 @@
         for t in range(WIN):
             tile = pl.ds(t * BLK, BLK)
             pt = jnp.exp2(s_scr[u, tile, wide] - top)
-            s_scr[u, tile, wide] = pt
             p_scr[u, tile, wide] = pt.astype(BF)
             norm = norm + jnp.sum(pt.reshape(16, 8, 256), axis=0)
         inv_norm = 1.0 / jnp.sum(norm, axis=0, keepdims=True)
@@ -215,7 +214,7 @@
     return inv_norms
 
 
-def dscores_of(u, inv_norms, ds_rows, vg, s_scr, dp_scr, ds_scr):
+def dscores_of(u, inv_norms, ds_rows, vg, p_scr, dp_scr, ds_scr):
     for hp in range(2):
         wide = pl.ds(hp * 256, 256)
         do2 = ds_rows[u, wide, :]
@@ -227,12 +226,13 @@
                 dpt = dp[(t - t0) * BLK : (t - t0 + 1) * BLK]
                 dp_scr[tile, wide] = dpt
                 mixed = mixed + jnp.sum(
-                    (s_scr[u, tile, wide] * dpt).reshape(16, 8, 256), axis=0
+                    (p_scr[u, tile, wide].astype(F32) * dpt).reshape(16, 8, 256), axis=0
                 )
         delta = jnp.sum(mixed, axis=0, keepdims=True) * inv_norms[hp]
         for t in range(WIN):
             tile = pl.ds(t * BLK, BLK)
-            ds_scr[u, tile, wide] = (s_scr[u, tile, wide] * (dp_scr[tile, wide] - delta)).astype(BF)
+            prob = p_scr[u, tile, wide].astype(F32)
+            ds_scr[u, tile, wide] = (prob * (dp_scr[tile, wide] - delta)).astype(BF)
 
 
 def query_grads(dq_ref, kg, ds_scr, norms):
@@ -434,11 +434,11 @@
         assemble(ctx, span_ref, 1, me.core, w_scr, dv.mine, part)
     gv.complete()
     window(ctx, 0, span_ref, inv, vbuf, vg)
-    dscores_of(0, norms[0], ds_rows, vg, s_scr, dp_scr, ds_scr)
+    dscores_of(0, norms[0], ds_rows, vg, p_scr, dp_scr, ds_scr)
     dv.first_leg()
     window_terms(0, ds_scr, qn, w_scr)
     window(ctx, 1, span_ref, inv, vbuf, vg)
-    dscores_of(1, norms[1], ds_rows, vg, s_scr, dp_scr, ds_scr)
+    dscores_of(1, norms[1], ds_rows, vg, p_scr, dp_scr, ds_scr)
     window_terms(1, ds_scr, qn, w_scr)
     for part in range(2):
         assemble(ctx, span_ref, 0, 1 - me.core, w_scr, dk.theirs, part)

time: 60.4 us -> 60.4 us (level)
  no operation moved by 1% of the time
where the time goes in v10:
time: 60.4 us; the launch traced here: 60 us
  Pallas kernels  59.3 us (98%)
  between operations  0.64 us (1%)
    pallas_call x1, Pallas kernels, per_device(): pl.pallas_call(kernel, out_shape=[jax.ShapeDtypeStruct((256, 512), BF), j...  56.9 us
    pallas_call x1, Pallas kernels, per_device(): pl.pallas_call(cast_kernel, out_shape=[jax.ShapeDtypeStruct((8, 2, BLK, H...  2.47 us

profile of v10, /device:TPU:8, one launch (start us, length us, event | category | flops | bytes accessed | tf_op | source)
XLA Modules:
  0.0 60.0 jit_solution(17508268486736512734)
XLA Ops:
  0.6 56.9 %backward.1 = (bf16[256,512]{1,0:T(8,128)(2,1)}, bf16[2,8,2,128,128]{4,3,2,1,0:T(8,128)(2,1)}) custom-call(bf16[256,512]{1,0:T(8,128)(2,1)} %q_ref.1, bf16[8,2,128,128]{3,2,1,0:T(8,128)(2,1)} %bitcast.5, bf16[8,2,128,128]{3,2,1,0:T(8,128)(2,1)} %bitcast.6, bf16[256,512]{1,0:T(8,128)(2,1)} %do_ref.1, s32[32]{0:T(128)} %span_ref.1, s32[32,128]{1,0:T(8,128)} %bitcast.7), custom_call_target="tpu_custom_call" | custom-call | tf_op jit(solution)/shard_map/backward/pallas_call | solution.py:496
  57.5 2.5 %widen.1 = (f32[8,2,128,128]{3,2,1,0:T(8,128)}, f32[8,2,128,128]{3,2,1,0:T(8,128)}, bf16[256,512]{1,0:T(8,128)(2,1)}) custom-call(bf16[2,8,2,128,128]{4,3,2,1,0:T(8,128)(2,1)} %get-tuple-element.8.result, bf16[256,512]{1,0:T(8,128)(2,1)} %get-tuple-element.9.dq_in), custom_call_target="tpu_custom_call" | custom-call | tf_op jit(solution)/shard_map/widen/pallas_call | solution.py:539

commit v11 on v7

--- a/solution.py
+++ b/solution.py
@@ -286,7 +286,7 @@
         for xx in range(4):
             mine[xx] = (mine[xx].astype(F32) + self.r0[xx].astype(F32)).astype(BF)
         self.leg1 = []
-        for i, d in enumerate((1, -1, 2)):
+        for i, d in enumerate((2, 1, -1)):
             x = (me.x + d + 4) % 4
             y = (me.y + d + 4) % 4
             self.leg1.append(
@@ -308,7 +308,7 @@
                 total = total + got[i].astype(F32)
             own[...] = total.astype(BF)
         self.leg2 = []
-        for i, d in enumerate((1, -1, 2)):
+        for i, d in enumerate((2, 1, -1)):
             x = (me.x + d + 4) % 4
             y = (me.y + d + 4) % 4
             self.leg2.append(

time: 60.1 us -> 60.1 us (level)
  no operation moved by 1% of the time
where the time goes in v11:
time: 60.1 us; the launch traced here: 59.9 us
  Pallas kernels  59.3 us (99%)
  between operations  0.64 us (1%)
    pallas_call x1, Pallas kernels, per_device(): pl.pallas_call(kernel, out_shape=[jax.ShapeDtypeStruct((256, 512), BF), j...  56.8 us
    pallas_call x1, Pallas kernels, per_device(): pl.pallas_call(cast_kernel, out_shape=[jax.ShapeDtypeStruct((8, 2, BLK, H...  2.47 us

profile of v11, /device:TPU:8, one launch (start us, length us, event | category | flops | bytes accessed | tf_op | source)
XLA Modules:
  0.0 59.9 jit_solution(2210124701088325695)
XLA Ops:
  0.6 56.8 %backward.1 = (bf16[256,512]{1,0:T(8,128)(2,1)}, bf16[2,8,2,128,128]{4,3,2,1,0:T(8,128)(2,1)}) custom-call(bf16[256,512]{1,0:T(8,128)(2,1)} %q_ref.1, bf16[8,2,128,128]{3,2,1,0:T(8,128)(2,1)} %bitcast.5, bf16[8,2,128,128]{3,2,1,0:T(8,128)(2,1)} %bitcast.6, bf16[256,512]{1,0:T(8,128)(2,1)} %do_ref.1, s32[32]{0:T(128)} %span_ref.1, s32[32,128]{1,0:T(8,128)} %bitcast.7), custom_call_target="tpu_custom_call" | custom-call | tf_op jit(solution)/shard_map/backward/pallas_call | solution.py:489
  57.4 2.5 %widen.1 = (f32[8,2,128,128]{3,2,1,0:T(8,128)}, f32[8,2,128,128]{3,2,1,0:T(8,128)}, bf16[256,512]{1,0:T(8,128)(2,1)}) custom-call(bf16[2,8,2,128,128]{4,3,2,1,0:T(8,128)(2,1)} %get-tuple-element.8.result, bf16[256,512]{1,0:T(8,128)(2,1)} %get-tuple-element.9.dq_in), custom_call_target="tpu_custom_call" | custom-call | tf_op jit(solution)/shard_map/widen/pallas_call | solution.py:532
